TPU v7x, 512 devices: a whole 4x4x16 slice. The times are simulated.
512 devices in a mesh: group: 32 (over y, x, core), tp: 16 (over z).
Axes of the slice: x: 4, y: 4, z: 16, core: 2. Of those that a mesh axis runs over, the one named last changes fastest.
Arguments:
- lengths: int32 [416], P('group'), may hold values from 1 to 510, as said below
- destination: int32 [416], replicated, may hold values from 0 to 415, as said below
- page_before: int32 [416, 4], P('group'), may hold values from 0 to 15, as said below
- page_after: int32 [416, 4], P('group'), may hold values from 0 to 15, as said below
- kv_cache: bfloat16 [32, 16, 16, 128, 256], P('group', 'tp'), may hold values from -8 to 8, as said below
- queries: bfloat16 [2, 416, 4096], P(None, 'group', 'tp'), may hold values from -32 to 32
- new_kv: bfloat16 [2, 416, 8, 256], P(None, 'group'), may hold values from -8 to 8, as said below
- residual: bfloat16 [2, 416, 5120], P(None, 'group'), may hold values from -16 to 16
- out_weight: bfloat16 [4096, 5120], P('tp'), may hold values from -0.5 to 0.5
- norm_gain: bfloat16 [5120], P('tp'), may hold values from 0.099609375 to 1.8984375
Outputs:
- kv_after: bfloat16 [32, 16, 16, 128, 256], P('group', 'tp')
- updated: bfloat16 [2, 416, 5120], P(None, 'group', 'tp')
- normed: bfloat16 [2, 416, 5120], P(None, 'group', 'tp')
Inputs may be any that keep to these rules, and one draw needn't show every extreme that they name: `lengths`: each row has ceil((length + 2) / 128) pages. `destination`: a permutation of the 416 positions; in each group exactly 11 rows go to other groups, no two of them to the same group, each of these rows has exactly 1 page, and the other rows stay in their group. `page_before`: for each group, the entries j below the page counts of its 13 rows (before the move) name each of its 16 slots once; other entries are not read. `page_after`: for each group, the entries j below the page counts of its 13 rows (after the move) name each of its 16 slots once; other entries are not read. `kv_cache`: entry [g, t] holds KV head t // 2 of group g, keys in the first 128 entries of a token and values in the last; entries t = 2k and 2k + 1 are equal. `new_kv`: keys then values of each KV head.
All inputs are finite; a program needn't handle non-finite values.
Results may differ from a plain program's by a relative error of at most 0.005.
Values may be sent and summed in bfloat16 or wider, within the bound.
A program may use at most 64 MiB of HBM per device.

v0:
```python
import jax
import jax.numpy as jnp
from jax import lax
from jax.sharding import PartitionSpec as P

PMOVE = 1


def on_device(
    lengths,
    destination,
    page_before,
    page_after,
    kv_cache,
    queries,
    new_kv,
    residual,
    out_weight,
    norm_gain,
):
    group_size = lax.axis_size("group")
    group_index = lax.axis_index("group")
    tp_index = lax.axis_index("tp")
    row_count = lengths.shape[0]
    own_pages = kv_cache[0, 0]
    slot_count = own_pages.shape[0]
    page_len = own_pages.shape[1]
    head_dim = own_pages.shape[2] // 2
    step_count = queries.shape[0]
    page_limit = page_before.shape[1]
    all_rows = destination.shape[0]
    row_ids = jnp.arange(row_count, dtype=jnp.int32)
    my_targets = lax.dynamic_slice_in_dim(destination, group_index * row_count, row_count)
    leaving = my_targets // row_count
    moving = leaving != group_index
    target_ids = jnp.arange(group_size, dtype=jnp.int32)
    chosen = moving[None, :] & (leaving[None, :] == target_ids[:, None])
    send_slots = jnp.sum(jnp.where(chosen[:, :, None], page_before[None, :, :PMOVE], 0), axis=1)
    send_pages = own_pages[send_slots]
    arrived = lax.all_to_all(send_pages, "group", split_axis=0, concat_axis=0, tiled=True)
    received = arrived.reshape(group_size * PMOVE, page_len, 2 * head_dim)
    after_ids = group_index * row_count + row_ids
    matches = destination[None, :] == after_ids[:, None]
    anchor = jnp.sum(jnp.where(matches, jnp.arange(all_rows, dtype=jnp.int32)[None, :], 0), axis=1)
    anchor_group = anchor // row_count
    anchor_local = anchor % row_count
    arrived_row = anchor_group != group_index
    page_ids = jnp.arange(page_limit, dtype=jnp.int32)
    needed = (lengths + step_count + page_len - 1) // page_len
    page_valid = page_ids[None, :] < needed[:, None]
    local_source = page_before[anchor_local]
    remote_source = (
        slot_count + anchor_group[:, None] * PMOVE + jnp.minimum(page_ids, PMOVE - 1)[None, :]
    )
    source = jnp.where(arrived_row[:, None], remote_source, local_source)
    target_slot = jnp.where(page_valid, page_after, slot_count).reshape(-1)
    source_of = (
        jnp.zeros((slot_count,), jnp.int32).at[target_slot].set(source.reshape(-1), mode="drop")
    )
    page_pool = jnp.concatenate([own_pages, received], axis=0)
    moved_pages = page_pool[source_of]
    positions = lengths[:, None] + jnp.arange(step_count, dtype=jnp.int32)[None, :]
    write_slot = jnp.take_along_axis(page_after, positions // page_len, axis=1)
    fresh_tokens = lax.dynamic_index_in_dim(new_kv, tp_index // 2, axis=2, keepdims=False)
    moved_pages = moved_pages.at[write_slot, positions % page_len].set(
        jnp.transpose(fresh_tokens, (1, 0, 2))
    )
    kv_after = moved_pages[None, None]
    row_grid = jnp.broadcast_to(row_ids[:, None], page_after.shape).reshape(-1)
    page_grid = jnp.broadcast_to(page_ids[None, :], page_after.shape).reshape(-1)
    slot_owner = jnp.zeros((slot_count,), jnp.int32).at[target_slot].set(row_grid, mode="drop")
    page_number = jnp.zeros((slot_count,), jnp.int32).at[target_slot].set(page_grid, mode="drop")
    token_pos = (
        page_number[:, None] * page_len + jnp.arange(page_len, dtype=jnp.int32)[None, :]
    ).reshape(-1)
    token_owner = jnp.repeat(slot_owner, page_len)
    flat_pages = moved_pages.reshape(slot_count * page_len, 2 * head_dim)
    cached_keys = flat_pages[:, :head_dim]
    cached_values = flat_pages[:, head_dim:]
    query_heads = queries.reshape(step_count, row_count, -1, head_dim)
    scores = jnp.einsum(
        "sahd,td->saht", query_heads, cached_keys, preferred_element_type=jnp.float32
    ) * head_dim ** (-0.5)
    step_ids = jnp.arange(step_count, dtype=jnp.int32)
    allowed = (token_owner[None, None, :] == row_ids[None, :, None]) & (
        token_pos[None, None, :] <= lengths[None, :, None] + step_ids[:, None, None]
    )
    scores = jnp.where(allowed[:, :, None, :], scores, -1e30)
    row_top = jnp.max(scores, axis=3, keepdims=True)
    weights = jnp.exp(scores - row_top)
    weight_total = jnp.sum(weights, axis=3, keepdims=True)
    mixed_heads = (
        jnp.einsum(
            "saht,td->sahd",
            weights.astype(jnp.bfloat16),
            cached_values,
            preferred_element_type=jnp.float32,
        )
        / weight_total
    )
    attention = mixed_heads.astype(jnp.bfloat16).reshape(step_count * row_count, -1)
    partial_value = jnp.dot(attention, out_weight, preferred_element_type=jnp.float32)
    col_width = norm_gain.shape[0]
    gain_values = norm_gain.astype(jnp.float32)
    residual_rows = residual.reshape(step_count * row_count, -1)
    whole_sum = lax.psum(partial_value, "tp")
    full_rows = residual_rows.astype(jnp.float32) + whole_sum
    mean_square = jnp.mean(full_rows * full_rows, axis=1)
    hidden = lax.dynamic_slice_in_dim(full_rows, tp_index * col_width, col_width, 1)
    updated = hidden.astype(jnp.bfloat16).reshape(step_count, row_count, col_width)
    normed = (
        (hidden * lax.rsqrt(mean_square + 1e-06)[:, None] * gain_values[None, :])
        .astype(jnp.bfloat16)
        .reshape(step_count, row_count, col_width)
    )
    return (kv_after, updated, normed)


def solution(mesh):
    in_specs = (
        P("group"),
        P(),
        P("group", None),
        P("group", None),
        P("group", "tp", None, None, None),
        P(None, "group", "tp"),
        P(None, "group", None, None),
        P(None, "group", None),
        P("tp", None),
        P("tp"),
    )
    out_specs = (P("group", "tp", None, None, None), P(None, "group", "tp"), P(None, "group", "tp"))
    return jax.shard_map(
        on_device, mesh=mesh, in_specs=in_specs, out_specs=out_specs, check_vma=False
    )
```

profile of v0, /device:TPU:6, one launch (start us, length us, event | category | flops | bytes accessed | tf_op | source)
XLA Modules:
  0.0 215.7 jit_solution(44666569801161759)
XLA Ops:
  7.2 0.0 copy-start
  7.2 0.8 slice_bitcast_fusion.4
  8.0 0.9 select_reduce_fusion
  8.9 0.8 broadcast_compare_fusion
  9.7 0.1 fusion.16
  9.8 3.3 %gather_fusion = bf16[32,128,256]{2,1,0:T(8,128)(2,1)} fusion(bf16[16,128,256]{2,1,0:T(8,128)(2,1)} %bitcast.54, s32[1024]{0:T(1024)S(1)} %pad_clamp_fusion.2), kind=kCustom, calls=%fused_computation | custom fusion | bytes 4194432 | tf_op jit(solution)/shard_map/gather | solution.py:39
  13.1 10.4 %all-to-all-start = ((bf16[32,1,128,256]{3,2,1,0:T(8,128)(2,1)}), bf16[32,1,128,256]{3,2,1,0:T(8,128)(2,1)}, u32[]{:S(2)}, u32[]{:S(2)}) async-start(bf16[32,1,128,256]{3,2,1,0:T(8,128)(2,1)} %bitcast.56), calls=%async_computation | async-start | bytes 4194304 | tf_op jit(solution)/shard_map/all_to_all | solution.py:40
  23.4 0.0 all-reduce.2.cloned.1.call-start
  23.5 0.1 copy.36
  23.6 0.1 shift-left_or_fusion
  23.8 0.1 copy.35
  23.9 0.1 reshape.502
  24.0 0.6 gather_fusion.1
  24.5 0.1 add_select_fusion.2
  24.6 0.1 reshape.545
  24.7 0.1 reshape.535
  24.8 0.8 gather_fusion.3
  25.7 0.1 gather.19
  25.7 0.1 fusion.9
  25.8 0.1 reshape.549
  25.9 0.9 constant_dynamic-slice_fusion
  27.0 0.1 reshape.567
  27.1 0.7 scatter_custom_fusion
  27.8 0.7 scatter_custom_fusion.3
  28.6 0.1 reshape.559
  28.7 0.7 scatter_custom_fusion.2
  29.5 0.1 add_bitcast_fusion
  29.5 0.1 broadcast_bitcast_fusion
  29.6 0.1 compare_and_fusion
  29.8 19.4 %all-to-all-done = bf16[32,1,128,256]{3,2,1,0:T(8,128)(2,1)} async-done(((bf16[32,1,128,256]{3,2,1,0:T(8,128)(2,1)}), bf16[32,1,128,256]{3,2,1,0:T(8,128)(2,1)}, u32[]{:S(2)}, u32[]{:S(2)}) %all-to-all-start) | async-done | bytes 2097184 | tf_op jit(solution)/shard_map/all_to_all | solution.py:40
  49.1 3.8 %pad_maximum_fusion = bf16[48,128,256]{2,1,0:T(8,128)(2,1)} fusion(bf16[32,128,256]{2,1,0:T(8,128)(2,1)} %bitcast.5, bf16[16,128,256]{2,1,0:T(8,128)(2,1)} %bitcast.55), kind=kLoop, calls=%fused_computation.8 | loop fusion | flops 1572864 | bytes 6291456 | tf_op jit(solution)/shard_map/concatenate | solution.py:60
  52.9 3.5 %gather_fusion.2 = bf16[16,128,256]{2,1,0:T(8,128)(2,1)} fusion(bf16[48,128,256]{2,1,0:T(8,128)(2,1)} %pad_maximum_fusion, s32[1024]{0:T(1024)S(1)} %pad_clamp_fusion), kind=kCustom, calls=%fused_computation.2 | custom fusion | bytes 2097216 | tf_op jit(solution)/shard_map/gather | solution.py:61
  56.4 4.1 %scatter_fusion = bf16[16,128,256]{2,1,0:T(8,128)(2,1)} fusion(bf16[16,128,256]{2,1,0:T(8,128)(2,1)} %gather_fusion.2, s32[26]{0:T(128)S(1)} %reshape.549, bf16[26,256]{1,0:T(8,128)(2,1)S(1)} %reshape.551), kind=kCustom, calls=%fused_computation.5 | custom fusion | bytes 40144 | tf_op jit(solution)/shard_map/scatter | solution.py:65
  60.5 1.4 fusion.27
  62.0 0.2 fusion.3
  62.2 0.0 copy-start.3
  62.2 1.4 fusion.2
  63.7 1.4 fusion.28
  65.1 0.0 all-reduce.2.cloned.1.call-update
  65.1 0.9 copy.38
  66.1 1.2 reshape.510
  67.2 137.2 %all-reduce.2.cloned.1.call-done = f32[26,5120]{1,0:T(8,128)} async-done(((f32[26,5120]{1,0:T(8,128)}), f32[26,5120]{1,0:T(8,128)}) %all-reduce.2.cloned.1.call-update) | async-done | bytes 532496 | tf_op jit(solution)/shard_map/psum | solution.py:106
  204.4 1.3 multiply_reduce_fusion
  205.7 0.8 copy-done.2
  206.5 0.1 dynamic-slice_convert_fusion
  206.6 0.6 copy.41
  207.2 0.9 multiply_convert_fusion
  208.2 0.6 copy.42
  (40 shorter events, 0.3 us)
Async XLA Ops:
  7.2 56.5 %copy-start = (bf16[256,5120]{1,0:T(8,128)(2,1)S(1)}, bf16[256,5120]{1,0:T(8,128)(2,1)}, u32[]{:S(2)}) copy-start(bf16[256,5120]{1,0:T(8,128)(2,1)} %param.18) | copy-start | bytes 7864324
  13.1 10.4 %copy-start.5 = (s32[13,4]{0,1:T(4,128)S(1)}, s32[13,4]{0,1:T(4,128)}, u32[]{:S(2)}) copy-start(s32[13,4]{0,1:T(4,128)} %param.12) | copy-start | bytes 628
  13.1 10.5 %copy-start.6 = (s32[13]{0:T(128)S(1)}, s32[13]{0:T(128)}, u32[]{:S(2)}) copy-start(s32[13]{0:T(128)} %param.10) | copy-start | bytes 160
  13.1 10.7 %copy-start.1 = (s32[13,4]{0,1:T(4,128)S(1)}, s32[13,4]{0,1:T(4,128)}, u32[]{:S(2)}) copy-start(s32[13,4]{0,1:T(4,128)} %param.13) | copy-start | bytes 628
  13.1 36.0 %all-to-all-start = ((bf16[32,1,128,256]{3,2,1,0:T(8,128)(2,1)}), bf16[32,1,128,256]{3,2,1,0:T(8,128)(2,1)}, u32[]{:S(2)}, u32[]{:S(2)}) async-start(bf16[32,1,128,256]{3,2,1,0:T(8,128)(2,1)} %bitcast.56), calls=%async_computation | async-start | bytes 4194304 | tf_op jit(solution)/shard_map/all_to_all | solution.py:40
  23.4 180.9 %all-reduce.2.cloned.1.call-start = ((), (), s32[]{:S(2)}) async-start(), calls=%async_computation.1 | async-start | bytes 1310720 | tf_op jit(solution)/shard_map/psum | solution.py:106
  24.8 2.1 copy-start.4
  62.2 2.9 %copy-start.3 = (bf16[2,13,5120]{2,0,1:T(2,128)(2,1)S(1)}, bf16[2,13,5120]{2,0,1:T(2,128)(2,1)}, u32[]{:S(2)}) copy-start(bf16[2,13,5120]{2,0,1:T(2,128)(2,1)} %param.17) | copy-start | bytes 798724
  63.7 3.6 %copy-start.7 = (bf16[320]{0:T(512)(128)(2,1)S(1)}, bf16[320]{0:T(512)(128)(2,1)}, u32[]{:S(2)}) copy-start(bf16[320]{0:T(512)(128)(2,1)} %param.19) | copy-start | bytes 1924
  205.7 0.8 copy-start.2
Sparse Core Ops, SparseCore 0:
  65.2 139.1 all-reduce.1
where the time goes:
time: 216 us
  waiting for transfers between devices  157 us (73%)
  local copies, waits for them, and re-layouts  21.6 us (10%)
  between operations  14.4 us (7%)
  starting transfers between devices  10.4 us (5%)
  other arithmetic  8.52 us (4%)
  matrix products  4.23 us (2%)
    psum x1, waiting for transfers between devices, on_device(): whole_sum = lax.psum(partial_value, 'tp')  137 us
    all_to_all x1, waiting for transfers between devices, on_device(): lax.all_to_all(send_pages, 'group', split_axis=0, concat_axis=0, tiled=True)  19.4 us
    all_to_all x1, starting transfers between devices, on_device(): lax.all_to_all(send_pages, 'group', split_axis=0, concat_axis=0, tiled=True)  10.4 us
  transfers between devices with their start and end apart: 2, of which 2 were waited for; matrix products, arithmetic and copies ran while one was open for 4% of the time, Pallas kernels for 0%

commit v1 on v0

v1 whole, which is shorter than its diff:
```python
import jax
import jax.numpy as jnp
from jax import lax
from jax.experimental import pallas as pl
from jax.experimental.pallas import tpu as pltpu
from jax.sharding import PartitionSpec as P

MESH = pl.DeviceIdType.MESH
NG = 32
NT = 16
ROWS = 13
STEPS = 2
SLOTS = 16
PAGE = 128
HD = 128
RP = 32
D = 5120
COLS = D // NT
BLK = 80
F32 = jnp.float32
BF16 = jnp.bfloat16

SLOT_TO, RET_SRC, B_SRC, B_STAY, OWN, NUM, A_SRC, A_STAY = 0, 32, 64, 80, 96, 112, 128, 144
TABLE = 160


def torus_offsets():
    found = []
    for ky in range(4):
        for kx in range(4):
            for kc in range(2):
                if (ky, kx, kc) != (0, 0, 0):
                    found.append((min(ky, 4 - ky) + min(kx, 4 - kx), ky, kx, kc))
    return sorted(found, key=lambda o: -o[0])


def group_at(g, ky, kx, kc):
    c, x, y = lax.rem(g, 2), lax.rem(g // 2, 4), g // 8
    return lax.rem(y + ky, 4) * 8 + lax.rem(x + kx, 4) * 2 + lax.rem(c + kc, 2)


def group_ahead(g, k):
    return group_at(g, k // 8, lax.rem(k // 2, 4), lax.rem(k, 2))


def group_behind(g, k):
    return group_at(g, 4 - k // 8, 4 - lax.rem(k // 2, 4), lax.rem(k, 2))


def route_kernel(
    lens_in, dest_in, pb_in, q_in, nkv_in, table, pack, mine, fresh,
    lens, dest, pb, q, nkv, anchor, build, sem,
):
    loads = [
        pltpu.make_async_copy(src, dst, sem.at[n])
        for n, (src, dst) in enumerate(
            ((dest_in, dest), (lens_in, lens), (pb_in, pb), (nkv_in, nkv), (q_in, q))
        )
    ]
    for load in loads:
        load.start()
    pack[...] = jnp.zeros_like(pack)
    build[...] = jnp.zeros_like(build)
    for load in loads:
        load.wait()
    g = lax.axis_index("group")
    head = lax.axis_index("tp") // 2
    base = g * ROWS

    def scan(b, carry):
        r = dest[b] - base
        anchor[jnp.where((r >= 0) & (r < ROWS), r, ROWS)] = b
        return carry

    lax.fori_loop(0, NG * ROWS, scan, 0, unroll=16)

    def clear(d, carry):
        table[SLOT_TO + d] = 0
        table[RET_SRC + d] = 0
        return carry

    lax.fori_loop(0, NG, clear, 0, unroll=8)

    def before(i, carry):
        to = dest[base + i]
        r = to - base
        stay = (r >= 0) & (r < ROWS)
        d = to // ROWS
        table[SLOT_TO + d] = pb[0, i]
        table[RET_SRC + d] = i
        table[B_SRC + i] = jnp.where(stay, r, d)
        table[B_STAY + i] = stay.astype(jnp.int32)
        length = lens[jnp.where(stay, r, 0)]
        need = jnp.where(stay, (length + (STEPS + PAGE - 1)) >> 7, 1)
        for j in range(4):
            @pl.when(j < need)
            def _():
                c = pb[j, i]
                table[OWN + c] = i
                table[NUM + c] = j
        return carry

    lax.fori_loop(0, ROWS, before, 0)

    rid = lax.broadcasted_iota(jnp.int32, (RP, 208), 0)
    cid = lax.broadcasted_iota(jnp.int32, (RP, 208), 1)
    pick = (cid == ((rid & 1) * ROWS + (rid >> 1)) * 8 + head) & (rid < STEPS * ROWS)
    tokens = jnp.dot(
        pick.astype(F32).astype(BF16),
        nkv[...].astype(F32).reshape(208, 2 * HD).astype(BF16),
        preferred_element_type=F32,
    )
    fresh[...] = tokens
    for r in range(ROWS):
        anc = anchor[r]
        loc = anc - base
        stay = (loc >= 0) & (loc < ROWS)
        home = anc // ROWS
        table[A_SRC + r] = jnp.where(stay, loc, home)
        table[A_STAY + r] = stay.astype(jnp.int32)
        asked = q[r].astype(F32)
        build[r, 0:2] = asked[:, :HD]
        build[r, 2:4] = asked[:, HD:]
        build[r, 4:6] = tokens[2 * r : 2 * r + 2, :HD]
        build[r, 6:8] = tokens[2 * r : 2 * r + 2, HD:]
        length = lens[r]
        build[r, 8:9] = jnp.full((1, HD), (length >> 7) * PAGE, jnp.int32).astype(F32)
        build[r, 9:10] = jnp.full((1, HD), length & (PAGE - 1), jnp.int32).astype(F32)
        packet = build[r].astype(BF16)
        mine[r] = packet
        pack[home] = packet


def layer_kernel(
    table, kv, pack, mine, w, res, gain,
    recv, upd, nrm,
    kvv, wv, res_win, res32, sbuf, pkt, qs, nks, nvs, lens, score,
    part, land1, half1, half2, land2, relay, back, back_out, back_in, hid, sq_own, sq_all,
    load_sem, page_send, page_recv, pkt_send, pkt_recv, back_send, back_recv,
    rs_send, rs_recv, sq_send, sq_recv,
):
    g = lax.axis_index("group")
    t = lax.axis_index("tp")
    parity = lax.rem(t, 2)
    get_kv = pltpu.make_async_copy(kv, kvv, load_sem.at[0])
    get_w = pltpu.make_async_copy(w, wv, load_sem.at[1])
    get_res = pltpu.make_async_copy(
        res.at[:, :, pl.ds(pl.multiple_of((t // 2) * 640, 128), 640)], res_win, load_sem.at[2]
    )
    get_kv.start()
    get_w.start()
    get_res.start()

    def at_z(o):
        return lax.rem(t + (o + NT), NT)

    barrier = pltpu.get_barrier_semaphore()

    def greet_group(k, carry):
        pl.semaphore_signal(
            barrier, inc=1, device_id=(group_ahead(g, k), t), device_id_type=MESH
        )
        return carry

    def greet_tp(k, carry):
        pl.semaphore_signal(
            barrier, inc=1, device_id=(g, lax.rem(t + k, NT)), device_id_type=MESH
        )
        return carry

    lax.fori_loop(1, NG, greet_group, 0)
    lax.fori_loop(1, NT, greet_tp, 0)
    pl.semaphore_wait(barrier, NG + NT - 2)

    def packet_copy(k):
        d = group_ahead(g, k)
        return pltpu.make_async_remote_copy(
            src_ref=pack.at[d], dst_ref=pkt.at[g],
            send_sem=pkt_send.at[k], recv_sem=pkt_recv.at[g],
            device_id=(d, t), device_id_type=MESH,
        )

    def packet_here(k):
        s = group_behind(g, k)
        return pltpu.make_async_remote_copy(
            src_ref=pack.at[s], dst_ref=pkt.at[s],
            send_sem=pkt_send.at[k], recv_sem=pkt_recv.at[s],
            device_id=(group_ahead(g, k), t), device_id_type=MESH,
        )

    def send_packet(k, carry):
        packet_copy(k).start()
        return carry

    def take_packet(k, carry):
        packet_here(k).wait()
        return carry

    lax.fori_loop(1, NG, send_packet, 0)
    get_kv.wait()

    offsets = torus_offsets()

    core = lax.rem(g, 2)

    def page_copy(n, landed):
        hops, ky, kx, kc = offsets[n]
        d = group_at(g, ky + core * (4 - 2 * ky), kx + core * (4 - 2 * kx), kc)
        back = 1 - core if kc == 0 else core
        s = group_at(g, ky + back * (4 - 2 * ky), kx + back * (4 - 2 * kx), kc) if landed else g
        return d, pltpu.make_async_remote_copy(
            src_ref=sbuf.at[n], dst_ref=recv.at[s],
            send_sem=page_send.at[n], recv_sem=page_recv.at[s],
            device_id=(d, t), device_id_type=MESH,
        )

    def send_pages(first, last):
        for n in range(first, last):
            d, copy = page_copy(n, False)
            sbuf[n] = kvv[table[SLOT_TO + d]]
            copy.start()

    send_pages(0, 3)

    get_res.wait()
    res32[...] = jnp.zeros_like(res32)
    for a in range(ROWS):
        res32[2 * a : 2 * a + 2, :] = res_win[a].astype(F32)
    qs[...] = jnp.zeros_like(qs)
    nks[...] = jnp.zeros_like(nks)
    nvs[...] = jnp.zeros_like(nvs)
    lens[...] = jnp.zeros_like(lens)
    lax.fori_loop(1, NG, take_packet, 0)
    send_pages(3, 6)

    for i in range(ROWS):
        at = table[B_SRC + i]
        stay = table[B_STAY + i]
        near = mine[at * stay].astype(F32)
        far = pkt[at * (1 - stay)].astype(F32)
        row = jnp.where(stay == 1, near, far)
        qs[2 * i : 2 * i + 2, :] = row[0:2]
        qs[RP + 2 * i : RP + 2 * i + 2, :] = row[2:4]
        nks[2 * i : 2 * i + 2, :] = row[4:6]
        nvs[2 * i : 2 * i + 2, :] = row[6:8]
        length = jnp.broadcast_to(row[8:9] + row[9:10], (2, HD))
        lens[2 * i : 2 * i + 2, :] = length
        lens[RP + 2 * i : RP + 2 * i + 2, :] = length

    qa = qs[...].astype(BF16)
    row_all = lax.broadcasted_iota(jnp.int32, (2 * RP, PAGE), 0) & (RP - 1)
    lane = lax.broadcasted_iota(jnp.int32, (2 * RP, PAGE), 1)
    row_b = row_all >> 1
    lane_f = lane.astype(F32)
    row_len = lens[...]
    sc = lax.dot_general(
        qa, nks[...].astype(BF16), (((1,), (1,)), ((), ())), preferred_element_type=F32
    ) * (HD**-0.5)
    sc = jnp.where(((lane >> 1) == row_b) & ((lane & 1) <= (row_all & 1)), sc, -1e30)
    score[SLOTS] = sc
    top = sc
    for c in range(SLOTS):
        sc = lax.dot_general(
            qa, kvv[c, :, :HD], (((1,), (1,)), ((), ())), preferred_element_type=F32
        ) * (HD**-0.5)
        pos = lane_f + (table[NUM + c] * PAGE).astype(F32)
        sc = jnp.where((row_b == table[OWN + c]) & (pos < row_len), sc, -1e30)
        score[c] = sc
        top = jnp.maximum(top, sc)
    send_pages(6, 9)
    top = jnp.max(top, axis=1, keepdims=True)
    weight = jnp.exp(score[SLOTS] - top)
    total = weight
    mixed = jnp.dot(weight.astype(BF16), nvs[...].astype(BF16), preferred_element_type=F32)
    for c in range(SLOTS):
        weight = jnp.exp(score[c] - top)
        total = total + weight
        mixed = mixed + jnp.dot(
            weight.astype(BF16), kvv[c, :, HD:], preferred_element_type=F32
        )
    mixed = mixed / jnp.sum(total, axis=1, keepdims=True)
    att = jnp.concatenate([mixed[:RP], mixed[RP:]], axis=1).astype(BF16)

    get_w.wait()
    send_pages(9, 11)
    low = lax.broadcasted_iota(jnp.int32, (16, 128), 1) < 64
    for i in range(NT // 2):
        out = jnp.dot(att, wv[:, 640 * i : 640 * i + 640], preferred_element_type=F32)
        mid = out[:, 256:384]
        part[2 * i, 0:32] = out[:, 0:128].astype(BF16)
        part[2 * i, 32:64] = out[:, 128:256].astype(BF16)
        part[2 * i, 64:80] = jnp.where(low, mid[:16], pltpu.roll(mid[16:], 64, 1)).astype(BF16)
        part[2 * i + 1, 0:32] = out[:, 384:512].astype(BF16)
        part[2 * i + 1, 32:64] = out[:, 512:640].astype(BF16)
        part[2 * i + 1, 64:80] = jnp.where(
            low, pltpu.roll(mid[:16], 64, 1), mid[16:]
        ).astype(BF16)

    def z_copy(n, src, dst, o):
        return pltpu.make_async_remote_copy(
            src_ref=src, dst_ref=dst, send_sem=rs_send.at[n], recv_sem=rs_recv.at[n],
            device_id=(g, at_z(o)), device_id_type=MESH,
        )

    first = {
        1: z_copy(1, part.at[at_z(-7)], land1.at[1], -2),
        5: z_copy(5, part.at[at_z(7)], land1.at[5], 2),
        8: z_copy(8, part.at[at_z(8), pl.ds(0, 48)], half1, -3),
        9: z_copy(9, part.at[at_z(8), pl.ds(48, 32)], half2, 3),
        0: z_copy(0, part.at[at_z(-6)], land1.at[0], -1),
        4: z_copy(4, part.at[at_z(6)], land1.at[4], 1),
        3: z_copy(3, part.at[at_z(-4)], land1.at[3], -2),
        7: z_copy(7, part.at[at_z(4)], land1.at[7], 2),
        2: z_copy(2, part.at[at_z(-3)], land1.at[2], -1),
        6: z_copy(6, part.at[at_z(3)], land1.at[6], 1),
        10: z_copy(10, part.at[at_z(-1)], land2.at[0], -1),
        11: z_copy(11, part.at[at_z(1)], land2.at[1], 1),
    }
    for copy in first.values():
        copy.start()
    send_pages(11, 15)
    second = [
        z_copy(12, relay.at[0], land2.at[2], -5),
        z_copy(13, relay.at[1], land2.at[3], 5),
        z_copy(14, relay.at[2], land2.at[4], -2),
        z_copy(15, relay.at[3], land2.at[5], 2),
    ]
    for n, o, a, b in ((2, -2, 2, 3), (3, 2, 6, 7)):
        first[a].wait_recv()
        first[b].wait_recv()
        relay[n] = (
            part[at_z(o)].astype(F32) + land1[a].astype(F32) + land1[b].astype(F32)
        ).astype(BF16)
        second[n].start()
    send_pages(15, 19)
    for n, o, a, b, c in ((0, -5, 0, 1, 8), (1, 5, 4, 5, 9)):
        first[a].wait_recv()
        first[b].wait_recv()
        first[c].wait_recv()
        whole = part[at_z(o)].astype(F32) + land1[a].astype(F32) + land1[b].astype(F32)
        if n == 0:
            relay[n, 0:48] = (whole[0:48] + half1[...].astype(F32)).astype(BF16)
            relay[n, 48:80] = whole[48:80].astype(BF16)
        else:
            relay[n, 0:48] = whole[0:48].astype(BF16)
            relay[n, 48:80] = (whole[48:80] + half2[...].astype(F32)).astype(BF16)
        second[n].start()
    send_pages(19, 23)
    acc = part[t].astype(F32)
    first[10].wait_recv()
    first[11].wait_recv()
    acc = acc + land2[0].astype(F32) + land2[1].astype(F32)
    for n in (2, 3, 0, 1):
        second[n].wait_recv()
        acc = acc + land2[2 + n].astype(F32)

    back[...] = jnp.zeros_like(back)
    tail = jnp.concatenate([acc[64:80], pltpu.roll(acc[64:80], 64, 1)], axis=0)
    for i in range(ROWS):
        back[i, 0:2] = acc[2 * i : 2 * i + 2]
        back[i, 2:4] = acc[32 + 2 * i : 34 + 2 * i]
        back[i, 4:6] = tail[2 * i : 2 * i + 2]

    def back_copy(k):
        d = group_ahead(g, k)
        return d, pltpu.make_async_remote_copy(
            src_ref=back_out.at[d], dst_ref=back_in.at[g],
            send_sem=back_send.at[k], recv_sem=back_recv.at[g],
            device_id=(d, t), device_id_type=MESH,
        )

    def send_back(k, carry):
        d, copy = back_copy(k)
        back_out[d] = back[table[RET_SRC + d]]
        copy.start()
        return carry

    def take_back(k, carry):
        s = group_behind(g, k)
        pltpu.make_async_remote_copy(
            src_ref=back_out.at[s], dst_ref=back_in.at[s],
            send_sem=back_send.at[k], recv_sem=back_recv.at[s],
            device_id=(group_ahead(g, k), t), device_id_type=MESH,
        ).wait()
        return carry

    lax.fori_loop(1, NG, send_back, 0)
    send_pages(23, 27)

    hid[...] = jnp.zeros_like(hid)
    lax.fori_loop(1, NG, take_back, 0)
    for r in range(ROWS):
        at = table[A_SRC + r]
        stay = table[A_STAY + r]
        row = jnp.where(stay == 1, back[at * stay], back_in[at * (1 - stay)])
        for j in range(3):
            hid[j, 2 * r : 2 * r + 2, :] = row[2 * j : 2 * j + 2]

    even = parity == 0
    mid = res32[:, 256:384]
    sum_a = hid[0] + jnp.where(even, res32[:, 0:128], res32[:, 384:512])
    sum_b = hid[1] + jnp.where(even, res32[:, 128:256], res32[:, 512:640])
    sum_h = hid[2] + jnp.where(even, mid, pltpu.roll(mid, 64, 1))
    own = lax.broadcasted_iota(jnp.int32, (RP, 128), 1) < 64
    sum_h = jnp.where(own, sum_h, 0.0)
    square = jnp.sum(sum_a * sum_a + sum_b * sum_b + sum_h * sum_h, axis=1, keepdims=True)
    diag = lax.broadcasted_iota(jnp.int32, (RP, 128), 0) == lax.broadcasted_iota(
        jnp.int32, (RP, 128), 1
    )
    sq_own[...] = jnp.sum(jnp.where(diag, square, 0.0), axis=0, keepdims=True)

    def square_copy(k):
        return pltpu.make_async_remote_copy(
            src_ref=sq_own, dst_ref=sq_all.at[k],
            send_sem=sq_send.at[k], recv_sem=sq_recv.at[k],
            device_id=(g, at_z(k)), device_id_type=MESH,
        )

    order = [8, 7, 9, 6, 10, 5, 11, 4, 12, 3, 13, 2, 14, 1, 15]
    for k in order:
        square_copy(k).start()
    send_pages(27, 31)
    tail = sum_h[:, 0:64]
    value = jnp.where(
        even,
        jnp.concatenate([sum_a, sum_b, tail], axis=1),
        jnp.concatenate([tail, sum_a, sum_b], axis=1),
    )
    for a in range(ROWS):
        upd[a] = value[2 * a : 2 * a + 2, :].astype(BF16)
    scaled = value * gain[...].astype(F32).reshape(1, COLS)
    whole = sq_own[...]
    for k in reversed(order):
        square_copy(k).wait()
        whole = whole + sq_all[k]
    inverse = lax.rsqrt(whole * (1.0 / D) + 1e-6)
    factor = jnp.sum(jnp.where(diag, inverse, 0.0), axis=1, keepdims=True)
    scaled = scaled * factor
    for a in range(ROWS):
        nrm[a] = scaled[2 * a : 2 * a + 2, :].astype(BF16)

    for copy in first.values():
        copy.wait_send()
    for copy in second:
        copy.wait_send()
    for n in range(NG - 1):
        page_copy(n, True)[1].wait()


def place_kernel(
    table, lens, pb, pa, kv, recv, fresh, upd_in, nrm_in, kva, upd, nrm, buf, page_sem, out_sem
):
    def fetch(r, carry):
        need = (lens[r] + (STEPS + PAGE - 1)) >> 7
        at = table[A_SRC + r]
        stay = table[A_STAY + r]
        for j in range(4):
            @pl.when((j < need) & (stay == 0))
            def _():
                c = pa[j, r]
                pltpu.make_async_copy(recv.at[at], buf.at[c], page_sem.at[c]).start()

            @pl.when((j < need) & (stay == 1))
            def _():
                c = pa[j, r]
                pltpu.make_async_copy(kv.at[pb[j, at]], buf.at[c], page_sem.at[c]).start()
        return carry

    lax.fori_loop(0, ROWS, fetch, 0)
    upd[...] = upd_in[...]
    nrm[...] = nrm_in[...]
    lane_row = lax.broadcasted_iota(jnp.int32, (16, 2 * HD), 0)
    for c in range(SLOTS):
        pltpu.make_async_copy(kv.at[0], buf.at[c], page_sem.at[c]).wait()

    def write(r, carry):
        for s in range(STEPS):
            p = lens[r] + s
            c = pa[p >> 7, r]
            e = p & (PAGE - 1)
            base = pl.multiple_of((e >> 4) << 4, 16)
            block = buf[c, pl.ds(base, 16), :].astype(F32)
            token = fresh[pl.ds(2 * r + s, 1), :]
            buf[c, pl.ds(base, 16), :] = jnp.where(
                lane_row == (e & 15), token, block
            ).astype(BF16)
        return carry

    lax.fori_loop(0, ROWS, write, 0)
    out = pltpu.make_async_copy(buf, kva, out_sem)
    out.start()
    out.wait()


VM = pl.BlockSpec(memory_space=pltpu.VMEM)
SM = pl.BlockSpec(memory_space=pltpu.SMEM)
HBM = pl.BlockSpec(memory_space=pltpu.HBM)
DMA = pltpu.SemaphoreType.DMA


def on_device(
    lengths, destination, page_before, page_after, kv_cache,
    queries, new_kv, residual, out_weight, norm_gain,
):
    kv = kv_cache[0, 0]
    pb, pa = page_before.T, page_after.T
    table, pack, mine, fresh = pl.pallas_call(
        route_kernel,
        out_shape=(
            jax.ShapeDtypeStruct((TABLE,), jnp.int32),
            jax.ShapeDtypeStruct((NG, 16, 128), BF16),
            jax.ShapeDtypeStruct((16, 16, 128), BF16),
            jax.ShapeDtypeStruct((RP, 2 * HD), F32),
        ),
        in_specs=[HBM] * 5,
        out_specs=(SM, VM, VM, VM),
        scratch_shapes=[
            pltpu.SMEM((ROWS,), jnp.int32),
            pltpu.SMEM((NG * ROWS,), jnp.int32),
            pltpu.SMEM((4, ROWS), jnp.int32),
            pltpu.VMEM((ROWS, STEPS, 2 * HD), BF16),
            pltpu.VMEM((STEPS, ROWS, 8, 2 * HD), BF16),
            pltpu.SMEM((ROWS + 1,), jnp.int32),
            pltpu.VMEM((ROWS, 16, 128), F32),
            DMA((5,)),
        ],
        compiler_params=pltpu.CompilerParams(vmem_limit_bytes=60 << 20),
        name="route",
    )(lengths, destination, pb, queries.transpose(1, 0, 2), new_kv)
    recv, upd, nrm = pl.pallas_call(
        layer_kernel,
        out_shape=(
            jax.ShapeDtypeStruct((NG, PAGE, 2 * HD), BF16),
            jax.ShapeDtypeStruct((ROWS, STEPS, COLS), BF16),
            jax.ShapeDtypeStruct((ROWS, STEPS, COLS), BF16),
        ),
        in_specs=[SM, HBM, HBM, VM, HBM, HBM, VM],
        out_specs=(HBM, VM, VM),
        scratch_shapes=[
            pltpu.VMEM((SLOTS, PAGE, 2 * HD), BF16),
            pltpu.VMEM((2 * HD, D), BF16),
            pltpu.VMEM((ROWS, STEPS, 640), BF16),
            pltpu.VMEM((RP, 640), F32),
            pltpu.VMEM((NG, PAGE, 2 * HD), BF16),
            pltpu.VMEM((NG, 16, 128), BF16),
            pltpu.VMEM((2 * RP, HD), F32),
            pltpu.VMEM((128, HD), F32),
            pltpu.VMEM((128, HD), F32),
            pltpu.VMEM((2 * RP, HD), F32),
            pltpu.VMEM((SLOTS + 1, 2 * RP, PAGE), F32),
            pltpu.VMEM((NT, BLK, 128), BF16),
            pltpu.VMEM((8, BLK, 128), BF16),
            pltpu.VMEM((48, 128), BF16),
            pltpu.VMEM((32, 128), BF16),
            pltpu.VMEM((6, BLK, 128), BF16),
            pltpu.VMEM((4, BLK, 128), BF16),
            pltpu.VMEM((16, 8, 128), F32),
            pltpu.VMEM((NG, 8, 128), F32),
            pltpu.VMEM((NG, 8, 128), F32),
            pltpu.VMEM((3, RP, 128), F32),
            pltpu.VMEM((1, 128), F32),
            pltpu.VMEM((NT, 1, 128), F32),
            DMA((3,)),
            DMA((NG,)),
            DMA((NG,)),
            DMA((NG,)),
            DMA((NG,)),
            DMA((NG,)),
            DMA((NG,)),
            DMA((16,)),
            DMA((16,)),
            DMA((NT,)),
            DMA((NT,)),
        ],
        compiler_params=pltpu.CompilerParams(
            collective_id=0, has_side_effects=True, vmem_limit_bytes=58 << 20
        ),
        name="layer",
    )(
        table, kv, pack, mine, out_weight, residual.transpose(1, 0, 2),
        norm_gain,
    )
    kva, upd, nrm = pl.pallas_call(
        place_kernel,
        out_shape=(
            jax.ShapeDtypeStruct((SLOTS, PAGE, 2 * HD), BF16),
            jax.ShapeDtypeStruct((ROWS, STEPS, COLS), BF16),
            jax.ShapeDtypeStruct((ROWS, STEPS, COLS), BF16),
        ),
        in_specs=[SM, SM, SM, SM, HBM, HBM, VM, VM, VM],
        out_specs=(HBM, VM, VM),
        scratch_shapes=[
            pltpu.VMEM((SLOTS, PAGE, 2 * HD), BF16),
            DMA((SLOTS,)),
            DMA(()),
        ],
        compiler_params=pltpu.CompilerParams(vmem_limit_bytes=60 << 20),
        name="place",
    )(table, lengths, pb, pa, kv, recv, fresh, upd, nrm)
    return kva[None, None], upd.transpose(1, 0, 2), nrm.transpose(1, 0, 2)


def solution(mesh):
    in_specs = (
        P("group"),
        P(),
        P("group", None),
        P("group", None),
        P("group", "tp", None, None, None),
        P(None, "group", "tp"),
        P(None, "group", None, None),
        P(None, "group", None),
        P("tp", None),
        P("tp"),
    )
    out_specs = (P("group", "tp", None, None, None), P(None, "group", "tp"), P(None, "group", "tp"))
    return jax.shard_map(
        on_device, mesh=mesh, in_specs=in_specs, out_specs=out_specs, check_vma=False
    )
```

time: 216 us -> 66.9 us (0.31)
  the two profiles are of different devices: /device:TPU:6 before, /device:TPU:1 now
where the time goes in v1:
time: 66.9 us; the launch traced here: 66.6 us
  Pallas kernels  66 us (99%)
    pallas_call x1, Pallas kernels, on_device(): pl.pallas_call(layer_kernel, out_shape=(jax.ShapeDtypeStruct((NG, PAGE, 2...  58.4 us
    pallas_call x1, Pallas kernels, on_device(): pl.pallas_call(place_kernel, out_shape=(jax.ShapeDtypeStruct((SLOTS, PAGE...  4.3 us
    pallas_call x1, Pallas kernels, on_device(): pl.pallas_call(route_kernel, out_shape=(jax.ShapeDtypeStruct((TABLE,), jn...  3.24 us

profile of v1, /device:TPU:1, one launch (start us, length us, event | category | flops | bytes accessed | tf_op | source)
XLA Modules:
  0.0 66.6 jit_solution(1982567130740686684)
XLA Ops:
  0.6 3.2 %route.1 = (s32[160]{0:T(256)}, bf16[32,16,128]{2,1,0:T(8,128)(2,1)}, bf16[16,16,128]{2,1,0:T(8,128)(2,1)}, f32[32,256]{1,0:T(8,128)}) custom-call(s32[13]{0:T(128)} %lens.1, s32[416]{0:T(512)} %dest_in.1, s32[4,13]{1,0:T(4,128)} %bitcast.12, bf16[13,2,256]{2,1,0:T(2,128)(2,1)} %bitcast.11, bf16[2,13,8,256]{3,2,1,0:T(8,128)(2,1)} %nkv_in.1), custom_call_target="tpu_custom_call" | custom-call | tf_op jit(solution)/shard_map/route/pallas_call | solution.py:507
  3.9 58.4 %layer.1 = (bf16[32,128,256]{2,1,0:T(8,128)(2,1)}, bf16[13,2,320]{2,1,0:T(2,128)(2,1)}, bf16[13,2,320]{2,1,0:T(2,128)(2,1)}) custom-call(s32[160]{0:T(256)} %get-tuple-element.13.table, bf16[16,128,256]{2,1,0:T(8,128)(2,1)} %bitcast.8, bf16[32,16,128]{2,1,0:T(8,128)(2,1)} %get-tuple-element.14.pack, bf16[16,16,128]{2,1,0:T(8,128)(2,1)} %get-tuple-element.15.mine, ...), custom_call_target="tpu_custom_call" | custom-call | tf_op jit(solution)/shard_map/layer/pallas_call | solution.py:530
  62.3 4.3 %place.1 = (bf16[16,128,256]{2,1,0:T(8,128)(2,1)}, bf16[13,2,320]{2,1,0:T(2,128)(2,1)}, bf16[13,2,320]{2,1,0:T(2,128)(2,1)}) custom-call(s32[160]{0:T(256)} %get-tuple-element.13.table, s32[13]{0:T(128)} %lens.1, s32[4,13]{1,0:T(4,128)} %bitcast.13, s32[4,13]{1,0:T(4,128)} %bitcast.14, bf16[16,128,256]{2,1,0:T(8,128)(2,1)} %bitcast.9, ...), custom_call_target="tpu_custom_call" | custom-call | tf_op jit(solution)/shard_map/place/pallas_call | solution.py:583

commit v2 on v1

--- a/solution.py
+++ b/solution.py
@@ -21,7 +21,10 @@
 BF16 = jnp.bfloat16
 
 SLOT_TO, RET_SRC, B_SRC, B_STAY, OWN, NUM, A_SRC, A_STAY = 0, 32, 64, 80, 96, 112, 128, 144
-TABLE = 160
+A_POS, ARRIVED = 160, 176
+TABLE = 192
+MOVED = 11
+HALF = PAGE // 2
 
 
 def torus_offsets():
@@ -32,19 +35,6 @@
                 if (ky, kx, kc) != (0, 0, 0):
                     found.append((min(ky, 4 - ky) + min(kx, 4 - kx), ky, kx, kc))
     return sorted(found, key=lambda o: -o[0])
-
-
-def group_at(g, ky, kx, kc):
-    c, x, y = lax.rem(g, 2), lax.rem(g // 2, 4), g // 8
-    return lax.rem(y + ky, 4) * 8 + lax.rem(x + kx, 4) * 2 + lax.rem(c + kc, 2)
-
-
-def group_ahead(g, k):
-    return group_at(g, k // 8, lax.rem(k // 2, 4), lax.rem(k, 2))
-
-
-def group_behind(g, k):
-    return group_at(g, 4 - k // 8, 4 - lax.rem(k // 2, 4), lax.rem(k, 2))
 
 
 def route_kernel(
@@ -111,6 +101,7 @@
         preferred_element_type=F32,
     )
     fresh[...] = tokens
+    count = 0
     for r in range(ROWS):
         anc = anchor[r]
         loc = anc - base
@@ -118,6 +109,9 @@
         home = anc // ROWS
         table[A_SRC + r] = jnp.where(stay, loc, home)
         table[A_STAY + r] = stay.astype(jnp.int32)
+        table[A_POS + r] = count
+        table[ARRIVED + count] = home
+        count = count + jnp.where(stay, 0, 1)
         asked = q[r].astype(F32)
         build[r, 0:2] = asked[:, :HD]
         build[r, 2:4] = asked[:, HD:]
@@ -133,10 +127,10 @@
 
 def layer_kernel(
     table, kv, pack, mine, w, res, gain,
-    recv, upd, nrm,
-    kvv, wv, res_win, res32, sbuf, pkt, qs, nks, nvs, lens, score,
+    moved, upd, nrm,
+    kvv, wv, res_win, res32, sbuf, recv, comp, pkt, qs, nks, nvs, lens, score,
     part, land1, half1, half2, land2, relay, back, back_out, back_in, hid, sq_own, sq_all,
-    load_sem, page_send, page_recv, pkt_send, pkt_recv, back_send, back_recv,
+    load_sem, keep_sem, swap_send, swap_recv, page_send, page_recv, pkt_send, pkt_recv, back_send, back_recv,
     rs_send, rs_recv, sq_send, sq_recv,
 ):
     g = lax.axis_index("group")
@@ -151,76 +145,51 @@
     get_w.start()
     get_res.start()
 
+    zs = [lax.rem(t + o, NT) for o in range(NT)]
+
     def at_z(o):
-        return lax.rem(t + (o + NT), NT)
+        return zs[o % NT]
+
+    core, x, y = lax.rem(g, 2), lax.rem(g // 2, 4), g // 8
+    ys = [lax.rem(y + k, 4) * 8 for k in range(4)]
+    xs = [lax.rem(x + k, 4) * 2 for k in range(4)]
+    cs = [core, 1 - core]
+    ys_to = [ys[k] + core * (ys[-k % 4] - ys[k]) for k in range(4)]
+    xs_to = [xs[k] + core * (xs[-k % 4] - xs[k]) for k in range(4)]
+    offsets = torus_offsets()
+    peers = [ys_to[ky] + xs_to[kx] + cs[kc] for _, ky, kx, kc in offsets]
 
     barrier = pltpu.get_barrier_semaphore()
-
-    def greet_group(k, carry):
-        pl.semaphore_signal(
-            barrier, inc=1, device_id=(group_ahead(g, k), t), device_id_type=MESH
-        )
-        return carry
-
-    def greet_tp(k, carry):
-        pl.semaphore_signal(
-            barrier, inc=1, device_id=(g, lax.rem(t + k, NT)), device_id_type=MESH
-        )
-        return carry
-
-    lax.fori_loop(1, NG, greet_group, 0)
-    lax.fori_loop(1, NT, greet_tp, 0)
+    for d in peers:
+        pl.semaphore_signal(barrier, inc=1, device_id=(d, t), device_id_type=MESH)
+    for o in range(1, NT):
+        pl.semaphore_signal(barrier, inc=1, device_id=(g, zs[o]), device_id_type=MESH)
     pl.semaphore_wait(barrier, NG + NT - 2)
 
-    def packet_copy(k):
-        d = group_ahead(g, k)
+    def group_copy(src, dst, send_sem, recv_sem, d):
         return pltpu.make_async_remote_copy(
-            src_ref=pack.at[d], dst_ref=pkt.at[g],
-            send_sem=pkt_send.at[k], recv_sem=pkt_recv.at[g],
+            src_ref=src, dst_ref=dst, send_sem=send_sem, recv_sem=recv_sem,
             device_id=(d, t), device_id_type=MESH,
         )
 
-    def packet_here(k):
-        s = group_behind(g, k)
-        return pltpu.make_async_remote_copy(
-            src_ref=pack.at[s], dst_ref=pkt.at[s],
-            send_sem=pkt_send.at[k], recv_sem=pkt_recv.at[s],
-            device_id=(group_ahead(g, k), t), device_id_type=MESH,
-        )
-
-    def send_packet(k, carry):
-        packet_copy(k).start()
-        return carry
-
-    def take_packet(k, carry):
-        packet_here(k).wait()
-        return carry
-
-    lax.fori_loop(1, NG, send_packet, 0)
+    def all_copies(src, dst, send_sem, recv_sem):
+        most = pl.ds(0, NG - 1)
+        return group_copy(src.at[most], dst.at[most], send_sem, recv_sem, peers[0])
+
+    for d in peers:
+        group_copy(pack.at[d], pkt.at[g], pkt_send, pkt_recv, d).start()
+    packets = all_copies(pack, pkt, pkt_send, pkt_recv)
     get_kv.wait()
 
-    offsets = torus_offsets()
-
-    core = lax.rem(g, 2)
-
-    def page_copy(n, landed):
-        hops, ky, kx, kc = offsets[n]
-        d = group_at(g, ky + core * (4 - 2 * ky), kx + core * (4 - 2 * kx), kc)
-        back = 1 - core if kc == 0 else core
-        s = group_at(g, ky + back * (4 - 2 * ky), kx + back * (4 - 2 * kx), kc) if landed else g
-        return d, pltpu.make_async_remote_copy(
-            src_ref=sbuf.at[n], dst_ref=recv.at[s],
-            send_sem=page_send.at[n], recv_sem=page_recv.at[s],
-            device_id=(d, t), device_id_type=MESH,
-        )
+    half = pl.ds(pl.multiple_of(parity * HALF, HALF), HALF)
 
     def send_pages(first, last):
         for n in range(first, last):
-            d, copy = page_copy(n, False)
-            sbuf[n] = kvv[table[SLOT_TO + d]]
-            copy.start()
-
-    send_pages(0, 3)
+            d = peers[n]
+            sbuf[n] = kvv[table[SLOT_TO + d], half, :]
+            group_copy(sbuf.at[n], recv.at[g], page_send, page_recv, d).start()
+
+    send_pages(0, 4)
 
     get_res.wait()
     res32[...] = jnp.zeros_like(res32)
@@ -230,8 +199,8 @@
     nks[...] = jnp.zeros_like(nks)
     nvs[...] = jnp.zeros_like(nvs)
     lens[...] = jnp.zeros_like(lens)
-    lax.fori_loop(1, NG, take_packet, 0)
-    send_pages(3, 6)
+    packets.wait_recv()
+    send_pages(4, 8)
 
     for i in range(ROWS):
         at = table[B_SRC + i]
@@ -267,7 +236,7 @@
         sc = jnp.where((row_b == table[OWN + c]) & (pos < row_len), sc, -1e30)
         score[c] = sc
         top = jnp.maximum(top, sc)
-    send_pages(6, 9)
+    send_pages(8, 13)
     top = jnp.max(top, axis=1, keepdims=True)
     weight = jnp.exp(score[SLOTS] - top)
     total = weight
@@ -282,7 +251,7 @@
     att = jnp.concatenate([mixed[:RP], mixed[RP:]], axis=1).astype(BF16)
 
     get_w.wait()
-    send_pages(9, 11)
+    send_pages(13, 17)
     low = lax.broadcasted_iota(jnp.int32, (16, 128), 1) < 64
     for i in range(NT // 2):
         out = jnp.dot(att, wv[:, 640 * i : 640 * i + 640], preferred_element_type=F32)
@@ -318,7 +287,7 @@
     }
     for copy in first.values():
         copy.start()
-    send_pages(11, 15)
+    send_pages(17, 24)
     second = [
         z_copy(12, relay.at[0], land2.at[2], -5),
         z_copy(13, relay.at[1], land2.at[3], 5),
@@ -332,7 +301,7 @@
             part[at_z(o)].astype(F32) + land1[a].astype(F32) + land1[b].astype(F32)
         ).astype(BF16)
         second[n].start()
-    send_pages(15, 19)
+    send_pages(24, 31)
     for n, o, a, b, c in ((0, -5, 0, 1, 8), (1, 5, 4, 5, 9)):
         first[a].wait_recv()
         first[b].wait_recv()
@@ -345,7 +314,23 @@
             relay[n, 0:48] = whole[0:48].astype(BF16)
             relay[n, 48:80] = (whole[48:80] + half2[...].astype(F32)).astype(BF16)
         second[n].start()
-    send_pages(19, 23)
+    pages = all_copies(sbuf, recv, page_send, page_recv)
+    pages.wait_recv()
+    for j in range(MOVED):
+        comp[j] = recv[table[ARRIVED + j]]
+
+    def swap_copy(n, first, count):
+        some = pl.ds(first, count)
+        return pltpu.make_async_remote_copy(
+            src_ref=comp.at[some], dst_ref=moved.at[some, half],
+            send_sem=swap_send.at[n], recv_sem=swap_recv.at[n],
+            device_id=(g, t + 1 - 2 * parity), device_id_type=MESH,
+        )
+
+    swaps = [swap_copy(0, 0, 6), swap_copy(1, 6, MOVED - 6)]
+    swaps[0].start()
+    keep = pltpu.make_async_copy(comp, moved.at[:, half], keep_sem)
+    keep.start()
     acc = part[t].astype(F32)
     first[10].wait_recv()
     first[11].wait_recv()
@@ -361,34 +346,14 @@
         back[i, 2:4] = acc[32 + 2 * i : 34 + 2 * i]
         back[i, 4:6] = tail[2 * i : 2 * i + 2]
 
-    def back_copy(k):
-        d = group_ahead(g, k)
-        return d, pltpu.make_async_remote_copy(
-            src_ref=back_out.at[d], dst_ref=back_in.at[g],
-            send_sem=back_send.at[k], recv_sem=back_recv.at[g],
-            device_id=(d, t), device_id_type=MESH,
-        )
-
-    def send_back(k, carry):
-        d, copy = back_copy(k)
+    for d in peers:
         back_out[d] = back[table[RET_SRC + d]]
-        copy.start()
-        return carry
-
-    def take_back(k, carry):
-        s = group_behind(g, k)
-        pltpu.make_async_remote_copy(
-            src_ref=back_out.at[s], dst_ref=back_in.at[s],
-            send_sem=back_send.at[k], recv_sem=back_recv.at[s],
-            device_id=(group_ahead(g, k), t), device_id_type=MESH,
-        ).wait()
-        return carry
-
-    lax.fori_loop(1, NG, send_back, 0)
-    send_pages(23, 27)
+        group_copy(back_out.at[d], back_in.at[g], back_send, back_recv, d).start()
+    returns = all_copies(back_out, back_in, back_send, back_recv)
+    swaps[1].start()
 
     hid[...] = jnp.zeros_like(hid)
-    lax.fori_loop(1, NG, take_back, 0)
+    returns.wait_recv()
     for r in range(ROWS):
         at = table[A_SRC + r]
         stay = table[A_STAY + r]
@@ -409,17 +374,16 @@
     )
     sq_own[...] = jnp.sum(jnp.where(diag, square, 0.0), axis=0, keepdims=True)
 
-    def square_copy(k):
-        return pltpu.make_async_remote_copy(
-            src_ref=sq_own, dst_ref=sq_all.at[k],
-            send_sem=sq_send.at[k], recv_sem=sq_recv.at[k],
-            device_id=(g, at_z(k)), device_id_type=MESH,
-        )
-
-    order = [8, 7, 9, 6, 10, 5, 11, 4, 12, 3, 13, 2, 14, 1, 15]
-    for k in order:
-        square_copy(k).start()
-    send_pages(27, 31)
+    for o in (8, 7, 9, 6, 10, 5, 11, 4, 12, 3, 13, 2, 14, 1, 15):
+        pltpu.make_async_remote_copy(
+            src_ref=sq_own, dst_ref=sq_all.at[o], send_sem=sq_send, recv_sem=sq_recv,
+            device_id=(g, zs[o]), device_id_type=MESH,
+        ).start()
+    most = pl.ds(1, NT - 1)
+    squares = pltpu.make_async_remote_copy(
+        src_ref=sq_all.at[most], dst_ref=sq_all.at[most], send_sem=sq_send, recv_sem=sq_recv,
+        device_id=(g, zs[1]), device_id_type=MESH,
+    )
     tail = sum_h[:, 0:64]
     value = jnp.where(
         even,
@@ -430,8 +394,8 @@
         upd[a] = value[2 * a : 2 * a + 2, :].astype(BF16)
     scaled = value * gain[...].astype(F32).reshape(1, COLS)
     whole = sq_own[...]
-    for k in reversed(order):
-        square_copy(k).wait()
+    squares.wait_recv()
+    for k in range(1, NT):
         whole = whole + sq_all[k]
     inverse = lax.rsqrt(whole * (1.0 / D) + 1e-6)
     factor = jnp.sum(jnp.where(diag, inverse, 0.0), axis=1, keepdims=True)
@@ -443,22 +407,35 @@
         copy.wait_send()
     for copy in second:
         copy.wait_send()
-    for n in range(NG - 1):
-        page_copy(n, True)[1].wait()
+    packets.wait_send()
+    returns.wait_send()
+    squares.wait_send()
+    pages.wait_send()
+    keep.wait()
+    for copy in swaps:
+        copy.wait()
 
 
 def place_kernel(
-    table, lens, pb, pa, kv, recv, fresh, upd_in, nrm_in, kva, upd, nrm, buf, page_sem, out_sem
+    table, lens, pb, pa, kv, moved, fresh, upd_in, nrm_in, kva, upd, nrm, buf, page_sem, out_sem
 ):
+    passed = [
+        pltpu.make_async_copy(upd_in, upd, out_sem.at[1]),
+        pltpu.make_async_copy(nrm_in, nrm, out_sem.at[2]),
+    ]
+    for copy in passed:
+        copy.start()
+
     def fetch(r, carry):
         need = (lens[r] + (STEPS + PAGE - 1)) >> 7
         at = table[A_SRC + r]
+        pos = table[A_POS + r]
         stay = table[A_STAY + r]
         for j in range(4):
             @pl.when((j < need) & (stay == 0))
             def _():
                 c = pa[j, r]
-                pltpu.make_async_copy(recv.at[at], buf.at[c], page_sem.at[c]).start()
+                pltpu.make_async_copy(moved.at[pos], buf.at[c], page_sem.at[c]).start()
 
             @pl.when((j < need) & (stay == 1))
             def _():
@@ -467,8 +444,6 @@
         return carry
 
     lax.fori_loop(0, ROWS, fetch, 0)
-    upd[...] = upd_in[...]
-    nrm[...] = nrm_in[...]
     lane_row = lax.broadcasted_iota(jnp.int32, (16, 2 * HD), 0)
     for c in range(SLOTS):
         pltpu.make_async_copy(kv.at[0], buf.at[c], page_sem.at[c]).wait()
@@ -487,8 +462,10 @@
         return carry
 
     lax.fori_loop(0, ROWS, write, 0)
-    out = pltpu.make_async_copy(buf, kva, out_sem)
+    out = pltpu.make_async_copy(buf, kva, out_sem.at[0])
     out.start()
+    for copy in passed:
+        copy.wait()
     out.wait()
 
 
@@ -527,10 +504,10 @@
         compiler_params=pltpu.CompilerParams(vmem_limit_bytes=60 << 20),
         name="route",
     )(lengths, destination, pb, queries.transpose(1, 0, 2), new_kv)
-    recv, upd, nrm = pl.pallas_call(
+    moved, upd, nrm = pl.pallas_call(
         layer_kernel,
         out_shape=(
-            jax.ShapeDtypeStruct((NG, PAGE, 2 * HD), BF16),
+            jax.ShapeDtypeStruct((MOVED, PAGE, 2 * HD), BF16),
             jax.ShapeDtypeStruct((ROWS, STEPS, COLS), BF16),
             jax.ShapeDtypeStruct((ROWS, STEPS, COLS), BF16),
         ),
@@ -541,7 +518,9 @@
             pltpu.VMEM((2 * HD, D), BF16),
             pltpu.VMEM((ROWS, STEPS, 640), BF16),
             pltpu.VMEM((RP, 640), F32),
-            pltpu.VMEM((NG, PAGE, 2 * HD), BF16),
+            pltpu.VMEM((NG, HALF, 2 * HD), BF16),
+            pltpu.VMEM((NG, HALF, 2 * HD), BF16),
+            pltpu.VMEM((MOVED, HALF, 2 * HD), BF16),
             pltpu.VMEM((NG, 16, 128), BF16),
             pltpu.VMEM((2 * RP, HD), F32),
             pltpu.VMEM((128, HD), F32),
@@ -561,16 +540,19 @@
             pltpu.VMEM((1, 128), F32),
             pltpu.VMEM((NT, 1, 128), F32),
             DMA((3,)),
-            DMA((NG,)),
-            DMA((NG,)),
-            DMA((NG,)),
-            DMA((NG,)),
-            DMA((NG,)),
-            DMA((NG,)),
+            DMA(()),
+            DMA((2,)),
+            DMA((2,)),
+            DMA(()),
+            DMA(()),
+            DMA(()),
+            DMA(()),
+            DMA(()),
+            DMA(()),
             DMA((16,)),
             DMA((16,)),
-            DMA((NT,)),
-            DMA((NT,)),
+            DMA(()),
+            DMA(()),
         ],
         compiler_params=pltpu.CompilerParams(
             collective_id=0, has_side_effects=True, vmem_limit_bytes=58 << 20
@@ -587,16 +569,16 @@
             jax.ShapeDtypeStruct((ROWS, STEPS, COLS), BF16),
             jax.ShapeDtypeStruct((ROWS, STEPS, COLS), BF16),
         ),
-        in_specs=[SM, SM, SM, SM, HBM, HBM, VM, VM, VM],
-        out_specs=(HBM, VM, VM),
+        in_specs=[SM, SM, SM, SM, HBM, HBM, VM, HBM, HBM],
+        out_specs=(HBM, HBM, HBM),
         scratch_shapes=[
             pltpu.VMEM((SLOTS, PAGE, 2 * HD), BF16),
             DMA((SLOTS,)),
-            DMA(()),
+            DMA((3,)),
         ],
         compiler_params=pltpu.CompilerParams(vmem_limit_bytes=60 << 20),
         name="place",
-    )(table, lengths, pb, pa, kv, recv, fresh, upd, nrm)
+    )(table, lengths, pb, pa, kv, moved, fresh, upd, nrm)
     return kva[None, None], upd.transpose(1, 0, 2), nrm.transpose(1, 0, 2)
 
 

time: 66.9 us -> 59.4 us (0.89)
  Pallas kernels: 66 us -> 58.5 us
    pallas_call x1, Pallas kernels: 58.4 us -> 51.6 us  [on_device(): pl.pallas_call(layer_kernel, out_shape=(jax.ShapeDtypeStruct((MOVED, PAGE...]
    pallas_call x1, Pallas kernels: 4.3 us -> 3.63 us  [on_device(): pl.pallas_call(place_kernel, out_shape=(jax.ShapeDtypeStruct((SLOTS, PAGE...]
where the time goes in v2:
time: 59.4 us; the launch traced here: 59.1 us
  Pallas kernels  58.5 us (98%)
  between operations  0.65 us (1%)
    pallas_call x1, Pallas kernels, on_device(): pl.pallas_call(layer_kernel, out_shape=(jax.ShapeDtypeStruct((MOVED, PAGE...  51.6 us
    pallas_call x1, Pallas kernels, on_device(): pl.pallas_call(place_kernel, out_shape=(jax.ShapeDtypeStruct((SLOTS, PAGE...  3.63 us
    pallas_call x1, Pallas kernels, on_device(): pl.pallas_call(route_kernel, out_shape=(jax.ShapeDtypeStruct((TABLE,), jn...  3.27 us

profile of v2, /device:TPU:1, one launch (start us, length us, event | category | flops | bytes accessed | tf_op | source)
XLA Modules:
  0.0 59.1 jit_solution(1880757287273069030)
XLA Ops:
  0.6 3.3 %route.1 = (s32[192]{0:T(256)}, bf16[32,16,128]{2,1,0:T(8,128)(2,1)}, bf16[16,16,128]{2,1,0:T(8,128)(2,1)}, f32[32,256]{1,0:T(8,128)}) custom-call(s32[13]{0:T(128)} %lens.1, s32[416]{0:T(512)} %dest_in.1, s32[4,13]{1,0:T(4,128)} %bitcast.12, bf16[13,2,256]{2,1,0:T(2,128)(2,1)} %bitcast.11, bf16[2,13,8,256]{3,2,1,0:T(8,128)(2,1)} %nkv_in.1), custom_call_target="tpu_custom_call" | custom-call | tf_op jit(solution)/shard_map/route/pallas_call | solution.py:484
  3.9 51.6 %layer.1 = (bf16[11,128,256]{2,1,0:T(8,128)(2,1)}, bf16[13,2,320]{2,1,0:T(2,128)(2,1)}, bf16[13,2,320]{2,1,0:T(2,128)(2,1)}) custom-call(s32[192]{0:T(256)} %get-tuple-element.13.table, bf16[16,128,256]{2,1,0:T(8,128)(2,1)} %bitcast.8, bf16[32,16,128]{2,1,0:T(8,128)(2,1)} %get-tuple-element.14.pack, bf16[16,16,128]{2,1,0:T(8,128)(2,1)} %get-tuple-element.15.mine, ...), custom_call_target="tpu_custom_call" | custom-call | tf_op jit(solution)/shard_map/layer/pallas_call | solution.py:507
  55.5 3.6 %place.1 = (bf16[16,128,256]{2,1,0:T(8,128)(2,1)}, bf16[13,2,320]{2,1,0:T(2,128)(2,1)}, bf16[13,2,320]{2,1,0:T(2,128)(2,1)}) custom-call(s32[192]{0:T(256)} %get-tuple-element.13.table, s32[13]{0:T(128)} %lens.1, s32[4,13]{1,0:T(4,128)} %bitcast.13, s32[4,13]{1,0:T(4,128)} %bitcast.14, bf16[16,128,256]{2,1,0:T(8,128)(2,1)} %bitcast.9, ...), custom_call_target="tpu_custom_call" | custom-call | tf_op jit(solution)/shard_map/place/pallas_call | solution.py:565

commit v3 on v2

--- a/solution.py
+++ b/solution.py
@@ -253,17 +253,19 @@
     get_w.wait()
     send_pages(13, 17)
     low = lax.broadcasted_iota(jnp.int32, (16, 128), 1) < 64
-    for i in range(NT // 2):
-        out = jnp.dot(att, wv[:, 640 * i : 640 * i + 640], preferred_element_type=F32)
+
+    def project(m):
+        pair = lax.rem(t // 2 + m, NT // 2)
+        columns = pl.ds(pl.multiple_of(pair * 640, 128), 640)
+        out = jnp.dot(att, wv[:, columns], preferred_element_type=F32)
         mid = out[:, 256:384]
-        part[2 * i, 0:32] = out[:, 0:128].astype(BF16)
-        part[2 * i, 32:64] = out[:, 128:256].astype(BF16)
-        part[2 * i, 64:80] = jnp.where(low, mid[:16], pltpu.roll(mid[16:], 64, 1)).astype(BF16)
-        part[2 * i + 1, 0:32] = out[:, 384:512].astype(BF16)
-        part[2 * i + 1, 32:64] = out[:, 512:640].astype(BF16)
-        part[2 * i + 1, 64:80] = jnp.where(
-            low, pltpu.roll(mid[:16], 64, 1), mid[16:]
-        ).astype(BF16)
+        left, right = 2 * pair, 2 * pair + 1
+        part[left, 0:32] = out[:, 0:128].astype(BF16)
+        part[left, 32:64] = out[:, 128:256].astype(BF16)
+        part[left, 64:80] = jnp.where(low, mid[:16], pltpu.roll(mid[16:], 64, 1)).astype(BF16)
+        part[right, 0:32] = out[:, 384:512].astype(BF16)
+        part[right, 32:64] = out[:, 512:640].astype(BF16)
+        part[right, 64:80] = jnp.where(low, pltpu.roll(mid[:16], 64, 1), mid[16:]).astype(BF16)
 
     def z_copy(n, src, dst, o):
         return pltpu.make_async_remote_copy(
@@ -285,8 +287,11 @@
         10: z_copy(10, part.at[at_z(-1)], land2.at[0], -1),
         11: z_copy(11, part.at[at_z(1)], land2.at[1], 1),
     }
-    for copy in first.values():
-        copy.start()
+    for pairs, ready in (((4, 3, 5), (1, 5, 8, 9, 0, 4)), ((2, 6, 1, 7), (3, 7, 2, 6)), ((0,), (10, 11))):
+        for m in pairs:
+            project(m)
+        for n in ready:
+            first[n].start()
     send_pages(17, 24)
     second = [
         z_copy(12, relay.at[0], land2.at[2], -5),
@@ -294,14 +299,6 @@
         z_copy(14, relay.at[2], land2.at[4], -2),
         z_copy(15, relay.at[3], land2.at[5], 2),
     ]
-    for n, o, a, b in ((2, -2, 2, 3), (3, 2, 6, 7)):
-        first[a].wait_recv()
-        first[b].wait_recv()
-        relay[n] = (
-            part[at_z(o)].astype(F32) + land1[a].astype(F32) + land1[b].astype(F32)
-        ).astype(BF16)
-        second[n].start()
-    send_pages(24, 31)
     for n, o, a, b, c in ((0, -5, 0, 1, 8), (1, 5, 4, 5, 9)):
         first[a].wait_recv()
         first[b].wait_recv()
@@ -314,6 +311,22 @@
             relay[n, 0:48] = whole[0:48].astype(BF16)
             relay[n, 48:80] = (whole[48:80] + half2[...].astype(F32)).astype(BF16)
         second[n].start()
+    for n, o, a, b in ((2, -2, 2, 3), (3, 2, 6, 7)):
+        first[a].wait_recv()
+        first[b].wait_recv()
+        relay[n] = (
+            part[at_z(o)].astype(F32) + land1[a].astype(F32) + land1[b].astype(F32)
+        ).astype(BF16)
+        second[n].start()
+    send_pages(24, 31)
+    acc = part[t].astype(F32)
+    first[10].wait_recv()
+    first[11].wait_recv()
+    acc = acc + land2[0].astype(F32) + land2[1].astype(F32)
+    for n in (2, 3):
+        second[n].wait_recv()
+        acc = acc + land2[2 + n].astype(F32)
+
     pages = all_copies(sbuf, recv, page_send, page_recv)
     pages.wait_recv()
     for j in range(MOVED):
@@ -327,15 +340,11 @@
             device_id=(g, t + 1 - 2 * parity), device_id_type=MESH,
         )
 
-    swaps = [swap_copy(0, 0, 6), swap_copy(1, 6, MOVED - 6)]
+    swaps = [swap_copy(0, 0, 3), swap_copy(1, 3, 4), swap_copy(2, 7, 4)]
     swaps[0].start()
     keep = pltpu.make_async_copy(comp, moved.at[:, half], keep_sem)
     keep.start()
-    acc = part[t].astype(F32)
-    first[10].wait_recv()
-    first[11].wait_recv()
-    acc = acc + land2[0].astype(F32) + land2[1].astype(F32)
-    for n in (2, 3, 0, 1):
+    for n in (0, 1):
         second[n].wait_recv()
         acc = acc + land2[2 + n].astype(F32)
 
@@ -379,6 +388,7 @@
             src_ref=sq_own, dst_ref=sq_all.at[o], send_sem=sq_send, recv_sem=sq_recv,
             device_id=(g, zs[o]), device_id_type=MESH,
         ).start()
+    swaps[2].start()
     most = pl.ds(1, NT - 1)
     squares = pltpu.make_async_remote_copy(
         src_ref=sq_all.at[most], dst_ref=sq_all.at[most], send_sem=sq_send, recv_sem=sq_recv,
@@ -541,8 +551,8 @@
             pltpu.VMEM((NT, 1, 128), F32),
             DMA((3,)),
             DMA(()),
-            DMA((2,)),
-            DMA((2,)),
+            DMA((3,)),
+            DMA((3,)),
             DMA(()),
             DMA(()),
             DMA(()),

time: 59.4 us -> 57.4 us (0.966)
  Pallas kernels: 58.5 us -> 56.4 us
    pallas_call x1, Pallas kernels: 51.6 us -> 49.5 us  [on_device(): pl.pallas_call(layer_kernel, out_shape=(jax.ShapeDtypeStruct((MOVED, PAGE...]
where the time goes in v3:
time: 57.4 us; the launch traced here: 57 us
  Pallas kernels  56.4 us (98%)
  between operations  0.65 us (1%)
    pallas_call x1, Pallas kernels, on_device(): pl.pallas_call(layer_kernel, out_shape=(jax.ShapeDtypeStruct((MOVED, PAGE...  49.5 us
    pallas_call x1, Pallas kernels, on_device(): pl.pallas_call(place_kernel, out_shape=(jax.ShapeDtypeStruct((SLOTS, PAGE...  3.61 us
    pallas_call x1, Pallas kernels, on_device(): pl.pallas_call(route_kernel, out_shape=(jax.ShapeDtypeStruct((TABLE,), jn...  3.27 us

profile of v3, /device:TPU:1, one launch (start us, length us, event | category | flops | bytes accessed | tf_op | source)
XLA Modules:
  0.0 57.0 jit_solution(10491388504721131738)
XLA Ops:
  0.6 3.3 %route.1 = (s32[192]{0:T(256)}, bf16[32,16,128]{2,1,0:T(8,128)(2,1)}, bf16[16,16,128]{2,1,0:T(8,128)(2,1)}, f32[32,256]{1,0:T(8,128)}) custom-call(s32[13]{0:T(128)} %lens.1, s32[416]{0:T(512)} %dest_in.1, s32[4,13]{1,0:T(4,128)} %bitcast.12, bf16[13,2,256]{2,1,0:T(2,128)(2,1)} %bitcast.11, bf16[2,13,8,256]{3,2,1,0:T(8,128)(2,1)} %nkv_in.1), custom_call_target="tpu_custom_call" | custom-call | tf_op jit(solution)/shard_map/route/pallas_call | solution.py:494
  3.9 49.5 %layer.1 = (bf16[11,128,256]{2,1,0:T(8,128)(2,1)}, bf16[13,2,320]{2,1,0:T(2,128)(2,1)}, bf16[13,2,320]{2,1,0:T(2,128)(2,1)}) custom-call(s32[192]{0:T(256)} %get-tuple-element.13.table, bf16[16,128,256]{2,1,0:T(8,128)(2,1)} %bitcast.8, bf16[32,16,128]{2,1,0:T(8,128)(2,1)} %get-tuple-element.14.pack, bf16[16,16,128]{2,1,0:T(8,128)(2,1)} %get-tuple-element.15.mine, ...), custom_call_target="tpu_custom_call" | custom-call | tf_op jit(solution)/shard_map/layer/pallas_call | solution.py:517
  53.4 3.6 %place.1 = (bf16[16,128,256]{2,1,0:T(8,128)(2,1)}, bf16[13,2,320]{2,1,0:T(2,128)(2,1)}, bf16[13,2,320]{2,1,0:T(2,128)(2,1)}) custom-call(s32[192]{0:T(256)} %get-tuple-element.13.table, s32[13]{0:T(128)} %lens.1, s32[4,13]{1,0:T(4,128)} %bitcast.13, s32[4,13]{1,0:T(4,128)} %bitcast.14, bf16[16,128,256]{2,1,0:T(8,128)(2,1)} %bitcast.9, ...), custom_call_target="tpu_custom_call" | custom-call | tf_op jit(solution)/shard_map/place/pallas_call | solution.py:575

commit v4 on v3

--- a/solution.py
+++ b/solution.py
@@ -24,7 +24,8 @@
 A_POS, ARRIVED = 160, 176
 TABLE = 192
 MOVED = 11
-HALF = PAGE // 2
+HALF = 48
+REST = PAGE - 2 * HALF
 
 
 def torus_offsets():
@@ -128,9 +129,9 @@
 def layer_kernel(
     table, kv, pack, mine, w, res, gain,
     moved, upd, nrm,
-    kvv, wv, res_win, res32, sbuf, recv, comp, pkt, qs, nks, nvs, lens, score,
+    kvv, wv, res_win, res32, sbuf, recv, comp, rest_out, rest_in, rest_kept, pkt, qs, nks, nvs, lens, score,
     part, land1, half1, half2, land2, relay, back, back_out, back_in, hid, sq_own, sq_all,
-    load_sem, keep_sem, swap_send, swap_recv, page_send, page_recv, pkt_send, pkt_recv, back_send, back_recv,
+    load_sem, keep_sem, swap_send, swap_recv, rest_send, rest_recv, page_send, page_recv, pkt_send, pkt_recv, back_send, back_recv,
     rs_send, rs_recv, sq_send, sq_recv,
 ):
     g = lax.axis_index("group")
@@ -181,13 +182,19 @@
     packets = all_copies(pack, pkt, pkt_send, pkt_recv)
     get_kv.wait()
 
-    half = pl.ds(pl.multiple_of(parity * HALF, HALF), HALF)
+    half = pl.ds(pl.multiple_of(parity * HALF, 16), HALF)
 
     def send_pages(first, last):
         for n in range(first, last):
             d = peers[n]
             sbuf[n] = kvv[table[SLOT_TO + d], half, :]
             group_copy(sbuf.at[n], recv.at[g], page_send, page_recv, d).start()
+
+    def send_rests(first, last):
+        for n in range(first, last):
+            d = peers[n]
+            rest_out[n] = kvv[table[SLOT_TO + d], 2 * HALF :, :]
+            group_copy(rest_out.at[n], rest_in.at[g], rest_send, rest_recv, d).start()
 
     send_pages(0, 4)
 
@@ -236,7 +243,7 @@
         sc = jnp.where((row_b == table[OWN + c]) & (pos < row_len), sc, -1e30)
         score[c] = sc
         top = jnp.maximum(top, sc)
-    send_pages(8, 13)
+    send_pages(8, 12)
     top = jnp.max(top, axis=1, keepdims=True)
     weight = jnp.exp(score[SLOTS] - top)
     total = weight
@@ -251,7 +258,6 @@
     att = jnp.concatenate([mixed[:RP], mixed[RP:]], axis=1).astype(BF16)
 
     get_w.wait()
-    send_pages(13, 17)
     low = lax.broadcasted_iota(jnp.int32, (16, 128), 1) < 64
 
     def project(m):
@@ -292,7 +298,7 @@
             project(m)
         for n in ready:
             first[n].start()
-    send_pages(17, 24)
+    send_pages(12, 22)
     second = [
         z_copy(12, relay.at[0], land2.at[2], -5),
         z_copy(13, relay.at[1], land2.at[3], 5),
@@ -318,7 +324,7 @@
             part[at_z(o)].astype(F32) + land1[a].astype(F32) + land1[b].astype(F32)
         ).astype(BF16)
         second[n].start()
-    send_pages(24, 31)
+    send_pages(22, 31)
     acc = part[t].astype(F32)
     first[10].wait_recv()
     first[11].wait_recv()
@@ -327,6 +333,21 @@
         second[n].wait_recv()
         acc = acc + land2[2 + n].astype(F32)
 
+    for n in (0, 1):
+        second[n].wait_recv()
+        acc = acc + land2[2 + n].astype(F32)
+
+    back[...] = jnp.zeros_like(back)
+    tail = jnp.concatenate([acc[64:80], pltpu.roll(acc[64:80], 64, 1)], axis=0)
+    for i in range(ROWS):
+        back[i, 0:2] = acc[2 * i : 2 * i + 2]
+        back[i, 2:4] = acc[32 + 2 * i : 34 + 2 * i]
+        back[i, 4:6] = tail[2 * i : 2 * i + 2]
+
+    for d in peers:
+        back_out[d] = back[table[RET_SRC + d]]
+        group_copy(back_out.at[d], back_in.at[g], back_send, back_recv, d).start()
+    returns = all_copies(back_out, back_in, back_send, back_recv)
     pages = all_copies(sbuf, recv, page_send, page_recv)
     pages.wait_recv()
     for j in range(MOVED):
@@ -340,26 +361,11 @@
             device_id=(g, t + 1 - 2 * parity), device_id_type=MESH,
         )
 
-    swaps = [swap_copy(0, 0, 3), swap_copy(1, 3, 4), swap_copy(2, 7, 4)]
+    swaps = [swap_copy(0, 0, 6), swap_copy(1, 6, MOVED - 6)]
     swaps[0].start()
-    keep = pltpu.make_async_copy(comp, moved.at[:, half], keep_sem)
+    keep = pltpu.make_async_copy(comp, moved.at[:, half], keep_sem.at[0])
     keep.start()
-    for n in (0, 1):
-        second[n].wait_recv()
-        acc = acc + land2[2 + n].astype(F32)
-
-    back[...] = jnp.zeros_like(back)
-    tail = jnp.concatenate([acc[64:80], pltpu.roll(acc[64:80], 64, 1)], axis=0)
-    for i in range(ROWS):
-        back[i, 0:2] = acc[2 * i : 2 * i + 2]
-        back[i, 2:4] = acc[32 + 2 * i : 34 + 2 * i]
-        back[i, 4:6] = tail[2 * i : 2 * i + 2]
-
-    for d in peers:
-        back_out[d] = back[table[RET_SRC + d]]
-        group_copy(back_out.at[d], back_in.at[g], back_send, back_recv, d).start()
-    returns = all_copies(back_out, back_in, back_send, back_recv)
-    swaps[1].start()
+    send_rests(0, 16)
 
     hid[...] = jnp.zeros_like(hid)
     returns.wait_recv()
@@ -388,7 +394,8 @@
             src_ref=sq_own, dst_ref=sq_all.at[o], send_sem=sq_send, recv_sem=sq_recv,
             device_id=(g, zs[o]), device_id_type=MESH,
         ).start()
-    swaps[2].start()
+    swaps[1].start()
+    send_rests(16, 31)
     most = pl.ds(1, NT - 1)
     squares = pltpu.make_async_remote_copy(
         src_ref=sq_all.at[most], dst_ref=sq_all.at[most], send_sem=sq_send, recv_sem=sq_recv,
@@ -420,8 +427,16 @@
     packets.wait_send()
     returns.wait_send()
     squares.wait_send()
+    rests = all_copies(rest_out, rest_in, rest_send, rest_recv)
+    rests.wait_recv()
+    for j in range(MOVED):
+        rest_kept[j] = rest_in[table[ARRIVED + j]]
+    keep_rest = pltpu.make_async_copy(rest_kept, moved.at[:, pl.ds(2 * HALF, REST)], keep_sem.at[1])
+    keep_rest.start()
     pages.wait_send()
+    rests.wait_send()
     keep.wait()
+    keep_rest.wait()
     for copy in swaps:
         copy.wait()
 
@@ -531,6 +546,9 @@
             pltpu.VMEM((NG, HALF, 2 * HD), BF16),
             pltpu.VMEM((NG, HALF, 2 * HD), BF16),
             pltpu.VMEM((MOVED, HALF, 2 * HD), BF16),
+            pltpu.VMEM((NG, REST, 2 * HD), BF16),
+            pltpu.VMEM((NG, REST, 2 * HD), BF16),
+            pltpu.VMEM((MOVED, REST, 2 * HD), BF16),
             pltpu.VMEM((NG, 16, 128), BF16),
             pltpu.VMEM((2 * RP, HD), F32),
             pltpu.VMEM((128, HD), F32),
@@ -550,9 +568,11 @@
             pltpu.VMEM((1, 128), F32),
             pltpu.VMEM((NT, 1, 128), F32),
             DMA((3,)),
-            DMA(()),
-            DMA((3,)),
-            DMA((3,)),
+            DMA((2,)),
+            DMA((2,)),
+            DMA((2,)),
+            DMA(()),
+            DMA(()),
             DMA(()),
             DMA(()),
             DMA(()),

time: 57.4 us -> 57.4 us (level)
  no operation moved by 1% of the time
where the time goes in v4:
time: 57.4 us; the launch traced here: 57.1 us
  Pallas kernels  56.4 us (98%)
  between operations  0.65 us (1%)
    pallas_call x1, Pallas kernels, on_device(): pl.pallas_call(layer_kernel, out_shape=(jax.ShapeDtypeStruct((MOVED, PAGE...  49.6 us
    pallas_call x1, Pallas kernels, on_device(): pl.pallas_call(place_kernel, out_shape=(jax.ShapeDtypeStruct((SLOTS, PAGE...  3.59 us
    pallas_call x1, Pallas kernels, on_device(): pl.pallas_call(route_kernel, out_shape=(jax.ShapeDtypeStruct((TABLE,), jn...  3.27 us

profile of v4, /device:TPU:1, one launch (start us, length us, event | category | flops | bytes accessed | tf_op | source)
XLA Modules:
  0.0 57.1 jit_solution(17050775885267125018)
XLA Ops:
  0.6 3.3 %route.1 = (s32[192]{0:T(256)}, bf16[32,16,128]{2,1,0:T(8,128)(2,1)}, bf16[16,16,128]{2,1,0:T(8,128)(2,1)}, f32[32,256]{1,0:T(8,128)}) custom-call(s32[13]{0:T(128)} %lens.1, s32[416]{0:T(512)} %dest_in.1, s32[4,13]{1,0:T(4,128)} %bitcast.12, bf16[13,2,256]{2,1,0:T(2,128)(2,1)} %bitcast.11, bf16[2,13,8,256]{3,2,1,0:T(8,128)(2,1)} %nkv_in.1), custom_call_target="tpu_custom_call" | custom-call | tf_op jit(solution)/shard_map/route/pallas_call | solution.py:509
  3.9 49.6 %layer.1 = (bf16[11,128,256]{2,1,0:T(8,128)(2,1)}, bf16[13,2,320]{2,1,0:T(2,128)(2,1)}, bf16[13,2,320]{2,1,0:T(2,128)(2,1)}) custom-call(s32[192]{0:T(256)} %get-tuple-element.13.table, bf16[16,128,256]{2,1,0:T(8,128)(2,1)} %bitcast.8, bf16[32,16,128]{2,1,0:T(8,128)(2,1)} %get-tuple-element.14.pack, bf16[16,16,128]{2,1,0:T(8,128)(2,1)} %get-tuple-element.15.mine, ...), custom_call_target="tpu_custom_call" | custom-call | tf_op jit(solution)/shard_map/layer/pallas_call | solution.py:532
  53.5 3.6 %place.1 = (bf16[16,128,256]{2,1,0:T(8,128)(2,1)}, bf16[13,2,320]{2,1,0:T(2,128)(2,1)}, bf16[13,2,320]{2,1,0:T(2,128)(2,1)}) custom-call(s32[192]{0:T(256)} %get-tuple-element.13.table, s32[13]{0:T(128)} %lens.1, s32[4,13]{1,0:T(4,128)} %bitcast.13, s32[4,13]{1,0:T(4,128)} %bitcast.14, bf16[16,128,256]{2,1,0:T(8,128)(2,1)} %bitcast.9, ...), custom_call_target="tpu_custom_call" | custom-call | tf_op jit(solution)/shard_map/place/pallas_call | solution.py:595

commit v5 on v3

--- a/solution.py
+++ b/solution.py
@@ -20,9 +20,8 @@
 F32 = jnp.float32
 BF16 = jnp.bfloat16
 
-SLOT_TO, RET_SRC, B_SRC, B_STAY, OWN, NUM, A_SRC, A_STAY = 0, 32, 64, 80, 96, 112, 128, 144
-A_POS, ARRIVED = 160, 176
-TABLE = 192
+A_SRC, A_STAY, A_POS = 0, 16, 32
+TABLE = 48
 MOVED = 11
 HALF = PAGE // 2
 
@@ -37,98 +36,11 @@
     return sorted(found, key=lambda o: -o[0])
 
 
-def route_kernel(
-    lens_in, dest_in, pb_in, q_in, nkv_in, table, pack, mine, fresh,
-    lens, dest, pb, q, nkv, anchor, build, sem,
-):
-    loads = [
-        pltpu.make_async_copy(src, dst, sem.at[n])
-        for n, (src, dst) in enumerate(
-            ((dest_in, dest), (lens_in, lens), (pb_in, pb), (nkv_in, nkv), (q_in, q))
-        )
-    ]
-    for load in loads:
-        load.start()
-    pack[...] = jnp.zeros_like(pack)
-    build[...] = jnp.zeros_like(build)
-    for load in loads:
-        load.wait()
-    g = lax.axis_index("group")
-    head = lax.axis_index("tp") // 2
-    base = g * ROWS
-
-    def scan(b, carry):
-        r = dest[b] - base
-        anchor[jnp.where((r >= 0) & (r < ROWS), r, ROWS)] = b
-        return carry
-
-    lax.fori_loop(0, NG * ROWS, scan, 0, unroll=16)
-
-    def clear(d, carry):
-        table[SLOT_TO + d] = 0
-        table[RET_SRC + d] = 0
-        return carry
-
-    lax.fori_loop(0, NG, clear, 0, unroll=8)
-
-    def before(i, carry):
-        to = dest[base + i]
-        r = to - base
-        stay = (r >= 0) & (r < ROWS)
-        d = to // ROWS
-        table[SLOT_TO + d] = pb[0, i]
-        table[RET_SRC + d] = i
-        table[B_SRC + i] = jnp.where(stay, r, d)
-        table[B_STAY + i] = stay.astype(jnp.int32)
-        length = lens[jnp.where(stay, r, 0)]
-        need = jnp.where(stay, (length + (STEPS + PAGE - 1)) >> 7, 1)
-        for j in range(4):
-            @pl.when(j < need)
-            def _():
-                c = pb[j, i]
-                table[OWN + c] = i
-                table[NUM + c] = j
-        return carry
-
-    lax.fori_loop(0, ROWS, before, 0)
-
-    rid = lax.broadcasted_iota(jnp.int32, (RP, 208), 0)
-    cid = lax.broadcasted_iota(jnp.int32, (RP, 208), 1)
-    pick = (cid == ((rid & 1) * ROWS + (rid >> 1)) * 8 + head) & (rid < STEPS * ROWS)
-    tokens = jnp.dot(
-        pick.astype(F32).astype(BF16),
-        nkv[...].astype(F32).reshape(208, 2 * HD).astype(BF16),
-        preferred_element_type=F32,
-    )
-    fresh[...] = tokens
-    count = 0
-    for r in range(ROWS):
-        anc = anchor[r]
-        loc = anc - base
-        stay = (loc >= 0) & (loc < ROWS)
-        home = anc // ROWS
-        table[A_SRC + r] = jnp.where(stay, loc, home)
-        table[A_STAY + r] = stay.astype(jnp.int32)
-        table[A_POS + r] = count
-        table[ARRIVED + count] = home
-        count = count + jnp.where(stay, 0, 1)
-        asked = q[r].astype(F32)
-        build[r, 0:2] = asked[:, :HD]
-        build[r, 2:4] = asked[:, HD:]
-        build[r, 4:6] = tokens[2 * r : 2 * r + 2, :HD]
-        build[r, 6:8] = tokens[2 * r : 2 * r + 2, HD:]
-        length = lens[r]
-        build[r, 8:9] = jnp.full((1, HD), (length >> 7) * PAGE, jnp.int32).astype(F32)
-        build[r, 9:10] = jnp.full((1, HD), length & (PAGE - 1), jnp.int32).astype(F32)
-        packet = build[r].astype(BF16)
-        mine[r] = packet
-        pack[home] = packet
-
-
 def layer_kernel(
-    table, kv, pack, mine, w, res, gain,
-    moved, upd, nrm,
-    kvv, wv, res_win, res32, sbuf, recv, comp, pkt, qs, nks, nvs, lens, score,
+    lens_in, dest_in, pb_in, q_in, nkv_in, kv, w, res, gain_in,
+    table, moved, upd_out, nrm_out, fresh_out,
+    length_of, dest, pb, dest_row, q, nkv, build, fresh, pack, slots,
+    mine, gain, upd, nrm, kvv, wv, res_win, res32, sbuf, recv, comp, pkt, qs, nks, nvs, lens, pages_of, score,
     part, land1, half1, half2, land2, relay, back, back_out, back_in, hid, sq_own, sq_all,
     load_sem, keep_sem, swap_send, swap_recv, page_send, page_recv, pkt_send, pkt_recv, back_send, back_recv,
     rs_send, rs_recv, sq_send, sq_recv,
@@ -141,7 +53,20 @@
     get_res = pltpu.make_async_copy(
         res.at[:, :, pl.ds(pl.multiple_of((t // 2) * 640, 128), 640)], res_win, load_sem.at[2]
     )
+    get_gain = pltpu.make_async_copy(gain_in, gain, load_sem.at[3])
+    small = [
+        pltpu.make_async_copy(src, dst, load_sem.at[4 + n])
+        for n, (src, dst) in enumerate(
+            (
+                (dest_in, dest_row), (dest_in, dest), (lens_in, length_of), (pb_in, pb),
+                (nkv_in, nkv), (q_in, q),
+            )
+        )
+    ]
+    for load in small:
+        load.start()
     get_kv.start()
+    get_gain.start()
     get_w.start()
     get_res.start()
 
@@ -164,6 +89,61 @@
         pl.semaphore_signal(barrier, inc=1, device_id=(d, t), device_id_type=MESH)
     for o in range(1, NT):
         pl.semaphore_signal(barrier, inc=1, device_id=(g, zs[o]), device_id_type=MESH)
+
+    build[...] = jnp.zeros_like(build)
+    for load in small:
+        load.wait()
+    base = g * ROWS
+    dest_all = dest_row[...].reshape(1, NG * ROWS)
+    lane = lax.broadcasted_iota(jnp.int32, (16, NG * ROWS), 1)
+    row = lax.broadcasted_iota(jnp.int32, (16, NG * ROWS), 0)
+    anchor = jnp.max(jnp.where(dest_all == base + row, lane, 0), axis=1, keepdims=True)
+    peer_row = lax.broadcasted_iota(jnp.int32, (NG, 1), 0)
+    peer_col = jnp.full((NG, 1), -1, jnp.int32)
+    for n, d in enumerate(peers):
+        peer_col = jnp.where(peer_row == n, d, peer_col)
+    lane = lax.broadcasted_iota(jnp.int32, (NG, NG * ROWS), 1)
+    taken = (lane >= base) & (lane < base + ROWS)
+    taken = taken & (dest_all >= peer_col * ROWS) & (dest_all < peer_col * ROWS + ROWS)
+    taker = jnp.max(jnp.where(taken, lane - base, 0), axis=1, keepdims=True)
+
+    rid = lax.broadcasted_iota(jnp.int32, (RP, 208), 0)
+    cid = lax.broadcasted_iota(jnp.int32, (RP, 208), 1)
+    pick = (cid == ((rid & 1) * ROWS + (rid >> 1)) * 8 + t // 2) & (rid < STEPS * ROWS)
+    tokens = jnp.dot(
+        pick.astype(F32).astype(BF16),
+        nkv[...].astype(F32).reshape(208, 2 * HD).astype(BF16),
+        preferred_element_type=F32,
+    )
+    fresh[...] = tokens
+    put_fresh = pltpu.make_async_copy(fresh, fresh_out, load_sem.at[10])
+    put_fresh.start()
+    lane = lax.broadcasted_iota(jnp.int32, (1, 128), 1)
+    homes = jnp.full((1, 128), -2, jnp.int32)
+    count = 0
+    for r in range(ROWS):
+        anc = anchor[r, 0]
+        loc = anc - base
+        stay = (loc >= 0) & (loc < ROWS)
+        home = anc // ROWS
+        homes = jnp.where(lane == r, home, homes)
+        table[A_SRC + r] = jnp.where(stay, loc, home)
+        table[A_STAY + r] = stay.astype(jnp.int32)
+        table[A_POS + r] = count
+        count = count + jnp.where(stay, 0, 1)
+        asked = q[r].astype(F32)
+        build[r, 0:2] = asked[:, :HD]
+        build[r, 2:4] = asked[:, HD:]
+        build[r, 4:6] = tokens[2 * r : 2 * r + 2, :HD]
+        build[r, 6:8] = tokens[2 * r : 2 * r + 2, HD:]
+        length = length_of[r]
+        build[r, 8:9] = jnp.full((1, HD), (length >> 7) * PAGE, jnp.int32).astype(F32)
+        build[r, 9:10] = jnp.full((1, HD), length & (PAGE - 1), jnp.int32).astype(F32)
+        mine[r] = build[r].astype(BF16)
+    giver = jnp.max(jnp.where(peer_col == homes, lane, 0), axis=1, keepdims=True)
+    for n in range(NG - 1):
+        pack[n] = mine[giver[n, 0]]
+        slots[n] = taker[n, 0]
     pl.semaphore_wait(barrier, NG + NT - 2)
 
     def group_copy(src, dst, send_sem, recv_sem, d):
@@ -176,8 +156,8 @@
         most = pl.ds(0, NG - 1)
         return group_copy(src.at[most], dst.at[most], send_sem, recv_sem, peers[0])
 
-    for d in peers:
-        group_copy(pack.at[d], pkt.at[g], pkt_send, pkt_recv, d).start()
+    for n, d in enumerate(peers):
+        group_copy(pack.at[n], pkt.at[g], pkt_send, pkt_recv, d).start()
     packets = all_copies(pack, pkt, pkt_send, pkt_recv)
     get_kv.wait()
 
@@ -186,7 +166,7 @@
     def send_pages(first, last):
         for n in range(first, last):
             d = peers[n]
-            sbuf[n] = kvv[table[SLOT_TO + d], half, :]
+            sbuf[n] = kvv[pb[0, slots[n]], half, :]
             group_copy(sbuf.at[n], recv.at[g], page_send, page_recv, d).start()
 
     send_pages(0, 4)
@@ -199,29 +179,35 @@
     nks[...] = jnp.zeros_like(nks)
     nvs[...] = jnp.zeros_like(nvs)
     lens[...] = jnp.zeros_like(lens)
+    pages_of[...] = jnp.full_like(pages_of, -1)
+    get_gain.wait()
     packets.wait_recv()
     send_pages(4, 8)
 
     for i in range(ROWS):
-        at = table[B_SRC + i]
-        stay = table[B_STAY + i]
-        near = mine[at * stay].astype(F32)
-        far = pkt[at * (1 - stay)].astype(F32)
-        row = jnp.where(stay == 1, near, far)
-        qs[2 * i : 2 * i + 2, :] = row[0:2]
-        qs[RP + 2 * i : RP + 2 * i + 2, :] = row[2:4]
-        nks[2 * i : 2 * i + 2, :] = row[4:6]
-        nvs[2 * i : 2 * i + 2, :] = row[6:8]
-        length = jnp.broadcast_to(row[8:9] + row[9:10], (2, HD))
-        lens[2 * i : 2 * i + 2, :] = length
-        lens[RP + 2 * i : RP + 2 * i + 2, :] = length
+        to = dest[base + i]
+        loc = to - base
+        stay = ((loc >= 0) & (loc < ROWS)).astype(jnp.int32)
+        near = mine[loc * stay].astype(F32)
+        far = pkt[(to // ROWS) * (1 - stay)].astype(F32)
+        got = jnp.where(stay == 1, near, far)
+        qs[2 * i : 2 * i + 2, :] = got[0:2]
+        qs[RP + 2 * i : RP + 2 * i + 2, :] = got[2:4]
+        nks[2 * i : 2 * i + 2, :] = got[4:6]
+        nvs[2 * i : 2 * i + 2, :] = got[6:8]
+        lens[2 * i : 2 * i + 2, :] = jnp.broadcast_to(got[8:9] + got[9:10], (2, HD))
+        need = 1 + stay * (((length_of[loc * stay] + (STEPS + PAGE - 1)) >> 7) - 1)
+        for j in range(4):
+            page = jnp.where(j < need, pb[j, i], -1)
+            pages_of[j, 2 * i : 2 * i + 2, :] = jnp.full((2, HD), page, jnp.int32)
 
     qa = qs[...].astype(BF16)
     row_all = lax.broadcasted_iota(jnp.int32, (2 * RP, PAGE), 0) & (RP - 1)
     lane = lax.broadcasted_iota(jnp.int32, (2 * RP, PAGE), 1)
     row_b = row_all >> 1
     lane_f = lane.astype(F32)
-    row_len = lens[...]
+    row_len = jnp.concatenate([lens[...], lens[...]], axis=0)
+    row_page = [jnp.concatenate([pages_of[j], pages_of[j]], axis=0) for j in range(4)]
     sc = lax.dot_general(
         qa, nks[...].astype(BF16), (((1,), (1,)), ((), ())), preferred_element_type=F32
     ) * (HD**-0.5)
@@ -232,8 +218,10 @@
         sc = lax.dot_general(
             qa, kvv[c, :, :HD], (((1,), (1,)), ((), ())), preferred_element_type=F32
         ) * (HD**-0.5)
-        pos = lane_f + (table[NUM + c] * PAGE).astype(F32)
-        sc = jnp.where((row_b == table[OWN + c]) & (pos < row_len), sc, -1e30)
+        held = jnp.zeros_like(row_len)
+        for j in range(4):
+            held = jnp.where(row_page[j] == c, row_len - j * PAGE, held)
+        sc = jnp.where(lane_f < held, sc, -1e30)
         score[c] = sc
         top = jnp.maximum(top, sc)
     send_pages(8, 13)
@@ -330,7 +318,11 @@
     pages = all_copies(sbuf, recv, page_send, page_recv)
     pages.wait_recv()
     for j in range(MOVED):
-        comp[j] = recv[table[ARRIVED + j]]
+        source = 0
+        for r in range(ROWS):
+            counts = (1 - table[A_STAY + r]) * (table[A_POS + r] == j).astype(jnp.int32)
+            source = source + counts * table[A_SRC + r]
+        comp[j] = recv[source]
 
     def swap_copy(n, first, count):
         some = pl.ds(first, count)
@@ -355,9 +347,9 @@
         back[i, 2:4] = acc[32 + 2 * i : 34 + 2 * i]
         back[i, 4:6] = tail[2 * i : 2 * i + 2]
 
-    for d in peers:
-        back_out[d] = back[table[RET_SRC + d]]
-        group_copy(back_out.at[d], back_in.at[g], back_send, back_recv, d).start()
+    for n, d in enumerate(peers):
+        back_out[n] = back[slots[n]]
+        group_copy(back_out.at[n], back_in.at[g], back_send, back_recv, d).start()
     returns = all_copies(back_out, back_in, back_send, back_recv)
     swaps[1].start()
 
@@ -402,6 +394,8 @@
     )
     for a in range(ROWS):
         upd[a] = value[2 * a : 2 * a + 2, :].astype(BF16)
+    put_upd = pltpu.make_async_copy(upd, upd_out, load_sem.at[0])
+    put_upd.start()
     scaled = value * gain[...].astype(F32).reshape(1, COLS)
     whole = sq_own[...]
     squares.wait_recv()
@@ -412,6 +406,8 @@
     scaled = scaled * factor
     for a in range(ROWS):
         nrm[a] = scaled[2 * a : 2 * a + 2, :].astype(BF16)
+    put_nrm = pltpu.make_async_copy(nrm, nrm_out, load_sem.at[1])
+    put_nrm.start()
 
     for copy in first.values():
         copy.wait_send()
@@ -424,6 +420,9 @@
     keep.wait()
     for copy in swaps:
         copy.wait()
+    put_fresh.wait()
+    put_upd.wait()
+    put_nrm.wait()
 
 
 def place_kernel(
@@ -439,18 +438,22 @@
     def fetch(r, carry):
         need = (lens[r] + (STEPS + PAGE - 1)) >> 7
         at = table[A_SRC + r]
-        pos = table[A_POS + r]
         stay = table[A_STAY + r]
-        for j in range(4):
-            @pl.when((j < need) & (stay == 0))
-            def _():
-                c = pa[j, r]
-                pltpu.make_async_copy(moved.at[pos], buf.at[c], page_sem.at[c]).start()
-
-            @pl.when((j < need) & (stay == 1))
-            def _():
+
+        @pl.when(stay == 0)
+        def _():
+            c = pa[0, r]
+            pltpu.make_async_copy(moved.at[table[A_POS + r]], buf.at[c], page_sem.at[c]).start()
+
+        @pl.when(stay == 1)
+        def _():
+            def page(j, carry):
                 c = pa[j, r]
                 pltpu.make_async_copy(kv.at[pb[j, at]], buf.at[c], page_sem.at[c]).start()
+                return carry
+
+            lax.fori_loop(0, need, page, 0)
+
         return carry
 
     lax.fori_loop(0, ROWS, fetch, 0)
@@ -458,17 +461,24 @@
     for c in range(SLOTS):
         pltpu.make_async_copy(kv.at[0], buf.at[c], page_sem.at[c]).wait()
 
+    def patch(r, s, p, both):
+        c = pa[p >> 7, r]
+        e = p & (PAGE - 1)
+        base = pl.multiple_of((e >> 4) << 4, 16)
+        block = buf[c, pl.ds(base, 16), :].astype(F32)
+        block = jnp.where(lane_row == (e & 15), fresh[pl.ds(2 * r + s, 1), :], block)
+        if both:
+            block = jnp.where(lane_row == (e & 15) + 1, fresh[pl.ds(2 * r + 1, 1), :], block)
+        buf[c, pl.ds(base, 16), :] = block.astype(BF16)
+
     def write(r, carry):
-        for s in range(STEPS):
-            p = lens[r] + s
-            c = pa[p >> 7, r]
-            e = p & (PAGE - 1)
-            base = pl.multiple_of((e >> 4) << 4, 16)
-            block = buf[c, pl.ds(base, 16), :].astype(F32)
-            token = fresh[pl.ds(2 * r + s, 1), :]
-            buf[c, pl.ds(base, 16), :] = jnp.where(
-                lane_row == (e & 15), token, block
-            ).astype(BF16)
+        p = lens[r]
+        patch(r, 0, p, True)
+
+        @pl.when((p & 15) == 15)
+        def _():
+            patch(r, 1, p + 1, False)
+
         return carry
 
     lax.fori_loop(0, ROWS, write, 0)
@@ -491,39 +501,32 @@
 ):
     kv = kv_cache[0, 0]
     pb, pa = page_before.T, page_after.T
-    table, pack, mine, fresh = pl.pallas_call(
-        route_kernel,
+    table, moved, upd, nrm, fresh = pl.pallas_call(
+        layer_kernel,
         out_shape=(
             jax.ShapeDtypeStruct((TABLE,), jnp.int32),
-            jax.ShapeDtypeStruct((NG, 16, 128), BF16),
-            jax.ShapeDtypeStruct((16, 16, 128), BF16),
+            jax.ShapeDtypeStruct((MOVED, PAGE, 2 * HD), BF16),
+            jax.ShapeDtypeStruct((ROWS, STEPS, COLS), BF16),
+            jax.ShapeDtypeStruct((ROWS, STEPS, COLS), BF16),
             jax.ShapeDtypeStruct((RP, 2 * HD), F32),
         ),
-        in_specs=[HBM] * 5,
-        out_specs=(SM, VM, VM, VM),
+        in_specs=[HBM] * 9,
+        out_specs=(SM, HBM, HBM, HBM, HBM),
         scratch_shapes=[
             pltpu.SMEM((ROWS,), jnp.int32),
             pltpu.SMEM((NG * ROWS,), jnp.int32),
             pltpu.SMEM((4, ROWS), jnp.int32),
+            pltpu.VMEM((NG * ROWS,), jnp.int32),
             pltpu.VMEM((ROWS, STEPS, 2 * HD), BF16),
             pltpu.VMEM((STEPS, ROWS, 8, 2 * HD), BF16),
-            pltpu.SMEM((ROWS + 1,), jnp.int32),
             pltpu.VMEM((ROWS, 16, 128), F32),
-            DMA((5,)),
-        ],
-        compiler_params=pltpu.CompilerParams(vmem_limit_bytes=60 << 20),
-        name="route",
-    )(lengths, destination, pb, queries.transpose(1, 0, 2), new_kv)
-    moved, upd, nrm = pl.pallas_call(
-        layer_kernel,
-        out_shape=(
-            jax.ShapeDtypeStruct((MOVED, PAGE, 2 * HD), BF16),
-            jax.ShapeDtypeStruct((ROWS, STEPS, COLS), BF16),
-            jax.ShapeDtypeStruct((ROWS, STEPS, COLS), BF16),
-        ),
-        in_specs=[SM, HBM, HBM, VM, HBM, HBM, VM],
-        out_specs=(HBM, VM, VM),
-        scratch_shapes=[
+            pltpu.VMEM((RP, 2 * HD), F32),
+            pltpu.VMEM((NG, 16, 128), BF16),
+            pltpu.SMEM((NG,), jnp.int32),
+            pltpu.VMEM((16, 16, 128), BF16),
+            pltpu.VMEM((COLS,), BF16),
+            pltpu.VMEM((ROWS, STEPS, COLS), BF16),
+            pltpu.VMEM((ROWS, STEPS, COLS), BF16),
             pltpu.VMEM((SLOTS, PAGE, 2 * HD), BF16),
             pltpu.VMEM((2 * HD, D), BF16),
             pltpu.VMEM((ROWS, STEPS, 640), BF16),
@@ -535,7 +538,8 @@
             pltpu.VMEM((2 * RP, HD), F32),
             pltpu.VMEM((128, HD), F32),
             pltpu.VMEM((128, HD), F32),
-            pltpu.VMEM((2 * RP, HD), F32),
+            pltpu.VMEM((RP, HD), F32),
+            pltpu.VMEM((4, RP, HD), jnp.int32),
             pltpu.VMEM((SLOTS + 1, 2 * RP, PAGE), F32),
             pltpu.VMEM((NT, BLK, 128), BF16),
             pltpu.VMEM((8, BLK, 128), BF16),
@@ -549,7 +553,7 @@
             pltpu.VMEM((3, RP, 128), F32),
             pltpu.VMEM((1, 128), F32),
             pltpu.VMEM((NT, 1, 128), F32),
-            DMA((3,)),
+            DMA((11,)),
             DMA(()),
             DMA((3,)),
             DMA((3,)),
@@ -569,8 +573,8 @@
         ),
         name="layer",
     )(
-        table, kv, pack, mine, out_weight, residual.transpose(1, 0, 2),
-        norm_gain,
+        lengths, destination, pb, queries.transpose(1, 0, 2), new_kv, kv, out_weight,
+        residual.transpose(1, 0, 2), norm_gain,
     )
     kva, upd, nrm = pl.pallas_call(
         place_kernel,

time: 57.4 us -> 53.7 us (0.936)
  Pallas kernels: 56.4 us -> 52.8 us
    pallas_call x2 -> x1, Pallas kernels: 52.8 us -> 49.3 us  [on_device(): pl.pallas_call(layer_kernel, out_shape=(jax.ShapeDtypeStruct((TABLE,), jn...]
where the time goes in v5:
time: 53.7 us; the launch traced here: 53.5 us
  Pallas kernels  52.8 us (98%)
  between operations  0.64 us (1%)
    pallas_call x1, Pallas kernels, on_device(): pl.pallas_call(layer_kernel, out_shape=(jax.ShapeDtypeStruct((TABLE,), jn...  49.3 us
    pallas_call x1, Pallas kernels, on_device(): pl.pallas_call(place_kernel, out_shape=(jax.ShapeDtypeStruct((SLOTS, PAGE...  3.49 us

profile of v5, /device:TPU:1, one launch (start us, length us, event | category | flops | bytes accessed | tf_op | source)
XLA Modules:
  0.0 53.5 jit_solution(4971043188528353287)
XLA Ops:
  0.6 49.3 %layer.1 = (s32[48]{0:T(128)}, bf16[11,128,256]{2,1,0:T(8,128)(2,1)}, bf16[13,2,320]{2,1,0:T(2,128)(2,1)}, bf16[13,2,320]{2,1,0:T(2,128)(2,1)}, f32[32,256]{1,0:T(8,128)}) custom-call(s32[13]{0:T(128)} %lens.1, s32[416]{0:T(512)} %dest_in.1, s32[4,13]{1,0:T(4,128)} %bitcast.12, bf16[13,2,256]{2,1,0:T(2,128)(2,1)} %bitcast.11, ...), custom_call_target="tpu_custom_call" | custom-call | tf_op jit(solution)/shard_map/layer/pallas_call | solution.py:504
  50.0 3.5 %place.1 = (bf16[16,128,256]{2,1,0:T(8,128)(2,1)}, bf16[13,2,320]{2,1,0:T(2,128)(2,1)}, bf16[13,2,320]{2,1,0:T(2,128)(2,1)}) custom-call(s32[48]{0:T(128)} %get-tuple-element.11.table, s32[13]{0:T(128)} %lens.1, s32[4,13]{1,0:T(4,128)} %bitcast.13, s32[4,13]{1,0:T(4,128)} %bitcast.14, bf16[16,128,256]{2,1,0:T(8,128)(2,1)} %bitcast.9, ...), custom_call_target="tpu_custom_call" | custom-call | tf_op jit(solution)/shard_map/place/pallas_call | solution.py:579

commit v6 on v5

--- a/solution.py
+++ b/solution.py
@@ -224,7 +224,7 @@
         sc = jnp.where(lane_f < held, sc, -1e30)
         score[c] = sc
         top = jnp.maximum(top, sc)
-    send_pages(8, 13)
+    send_pages(8, 12)
     top = jnp.max(top, axis=1, keepdims=True)
     weight = jnp.exp(score[SLOTS] - top)
     total = weight
@@ -239,7 +239,6 @@
     att = jnp.concatenate([mixed[:RP], mixed[RP:]], axis=1).astype(BF16)
 
     get_w.wait()
-    send_pages(13, 17)
     low = lax.broadcasted_iota(jnp.int32, (16, 128), 1) < 64
 
     def project(m):
@@ -280,7 +279,7 @@
             project(m)
         for n in ready:
             first[n].start()
-    send_pages(17, 24)
+    send_pages(12, 22)
     second = [
         z_copy(12, relay.at[0], land2.at[2], -5),
         z_copy(13, relay.at[1], land2.at[3], 5),
@@ -306,7 +305,7 @@
             part[at_z(o)].astype(F32) + land1[a].astype(F32) + land1[b].astype(F32)
         ).astype(BF16)
         second[n].start()
-    send_pages(24, 31)
+    send_pages(22, 31)
     acc = part[t].astype(F32)
     first[10].wait_recv()
     first[11].wait_recv()

time: 53.7 us -> 53.7 us (level)
  no operation moved by 1% of the time
where the time goes in v6:
time: 53.7 us; the launch traced here: 53.4 us
  Pallas kernels  52.8 us (98%)
  between operations  0.64 us (1%)
    pallas_call x1, Pallas kernels, on_device(): pl.pallas_call(layer_kernel, out_shape=(jax.ShapeDtypeStruct((TABLE,), jn...  49.3 us
    pallas_call x1, Pallas kernels, on_device(): pl.pallas_call(place_kernel, out_shape=(jax.ShapeDtypeStruct((SLOTS, PAGE...  3.48 us

profile of v6, /device:TPU:1, one launch (start us, length us, event | category | flops | bytes accessed | tf_op | source)
XLA Modules:
  0.0 53.4 jit_solution(14270032605275304858)
XLA Ops:
  0.6 49.3 %layer.1 = (s32[48]{0:T(128)}, bf16[11,128,256]{2,1,0:T(8,128)(2,1)}, bf16[13,2,320]{2,1,0:T(2,128)(2,1)}, bf16[13,2,320]{2,1,0:T(2,128)(2,1)}, f32[32,256]{1,0:T(8,128)}) custom-call(s32[13]{0:T(128)} %lens.1, s32[416]{0:T(512)} %dest_in.1, s32[4,13]{1,0:T(4,128)} %bitcast.12, bf16[13,2,256]{2,1,0:T(2,128)(2,1)} %bitcast.11, ...), custom_call_target="tpu_custom_call" | custom-call | tf_op jit(solution)/shard_map/layer/pallas_call | solution.py:503
  50.0 3.5 %place.1 = (bf16[16,128,256]{2,1,0:T(8,128)(2,1)}, bf16[13,2,320]{2,1,0:T(2,128)(2,1)}, bf16[13,2,320]{2,1,0:T(2,128)(2,1)}) custom-call(s32[48]{0:T(128)} %get-tuple-element.11.table, s32[13]{0:T(128)} %lens.1, s32[4,13]{1,0:T(4,128)} %bitcast.13, s32[4,13]{1,0:T(4,128)} %bitcast.14, bf16[16,128,256]{2,1,0:T(8,128)(2,1)} %bitcast.9, ...), custom_call_target="tpu_custom_call" | custom-call | tf_op jit(solution)/shard_map/place/pallas_call | solution.py:578
